TPU v7x, 128 devices: a whole 4x4x4 slice. The times are simulated.
128 devices in a mesh: gz: 2 (over core), gx: 32 (over z, y, x_hi), gy: 2 (over x_lo).
Axes of the slice: x: 4 (x_hi: 2, x_lo: 2; x = x_hi * 2 + x_lo), y: 4, z: 4, core: 2. Of those that a mesh axis runs over, the one named last changes fastest.
Arguments:
- prediction: float32 [64, 512, 256], P('gz', 'gx', 'gy'), may hold values from 0.01 to 0.99
- label: float32 [64, 512, 256], P('gz', 'gx', 'gy'), may hold values from 0.001 to 1
Outputs:
- loss: float32 [], replicated
- pred_grad: float32 [64, 512, 256], P('gz', 'gx', 'gy')
All inputs are finite; a program needn't handle non-finite values.
Results may differ from a plain program's by a relative error of at most 0.0003.
Values sent between devices are 32-bit elements; how exact they have to be, the bound alone decides.
A program may use at most 128 MiB of HBM per device.

v0:
```python
import jax
import jax.numpy as jnp
from jax import lax
from jax.sharding import PartitionSpec as P

ITERS = 5


def with_halo(x, sides, width):
    for axis, dim in sides:
        size, length = (lax.axis_size(axis), x.shape[dim])
        up = [(i, (i + 1) % size) for i in range(size - 1)]
        down = [(j, i) for i, j in up]
        last = lax.slice_in_dim(x, length - width, length, axis=dim)
        first = lax.slice_in_dim(x, 0, width, axis=dim)
        before = lax.ppermute(last, axis, up)
        after = lax.ppermute(first, axis, down)
        x = jnp.concatenate([before, x, after], axis=dim)
    return x


def passed_along(x, axis, by):
    length = lax.axis_size(axis)
    pairs = [(i, i + by) for i in range(length) if 0 <= i + by < length]
    return lax.ppermute(x, axis, pairs)


def pick(padded, dim, larger):
    count = padded.shape[dim] - 2
    lower = lax.slice_in_dim(padded, 0, count, axis=dim)
    centre = lax.slice_in_dim(padded, 1, count + 1, axis=dim)
    upper = lax.slice_in_dim(padded, 2, count + 2, axis=dim)
    if larger:
        take_low = lower > centre
    else:
        take_low = lower < centre
    best = jnp.where(take_low, lower, centre)
    code = jnp.where(take_low, 1, 0)
    if larger:
        take_up = upper > best
    else:
        take_up = upper < best
    best = jnp.where(take_up, upper, best)
    code = jnp.where(take_up, 2, code).astype(jnp.int32)
    return (best, code)


def rim_mask(shape, dim, index, count):
    place = lax.broadcasted_iota(jnp.int32, shape, dim)
    return (place == 0) & (index == 0) | (place == shape[dim] - 1) & (index == count - 1)


def fill_outer(extended):
    shape = extended.shape
    outside = rim_mask(shape, 1, lax.axis_index("gz"), lax.axis_size("gz"))
    outside = outside | rim_mask(shape, 2, lax.axis_index("gx"), lax.axis_size("gx"))
    outside = outside | rim_mask(shape, 3, lax.axis_index("gy"), lax.axis_size("gy"))
    return jnp.where(outside, jnp.float32(2.0), extended)


def erode(fields):
    extended = with_halo(fields, (("gz", 1), ("gx", 2), ("gy", 3)), 1)
    extended = fill_outer(extended)
    depth_min, depth_code = pick(extended[:, :, 1:-1, 1:-1], 1, False)
    rows_min, rows_code = pick(extended[:, 1:-1, :, 1:-1], 2, False)
    cols_min, cols_code = pick(extended[:, 1:-1, 1:-1, :], 3, False)
    take_rows = rows_min < depth_min
    best = jnp.where(take_rows, rows_min, depth_min)
    select = jnp.where(take_rows, 1, 0)
    take_cols = cols_min < best
    best = jnp.where(take_cols, cols_min, best)
    select = jnp.where(take_cols, 2, select).astype(jnp.int32)
    return (best, (depth_code, rows_code, cols_code, select))


def dilate(fields):
    first, first_code = pick(with_halo(fields, (("gz", 1),), 1), 1, True)
    second, second_code = pick(with_halo(first, (("gx", 2),), 1), 2, True)
    third, third_code = pick(with_halo(second, (("gy", 3),), 1), 3, True)
    return (third, (first_code, second_code, third_code))


def split_grad(grad, code):
    zeros = jnp.zeros_like(grad)
    keep = jnp.where(code == 0, grad, zeros)
    lower = jnp.where(code == 1, grad, zeros)
    upper = jnp.where(code == 2, grad, zeros)
    return (keep, lower, upper)


def join_grad(keep, lower, upper, from_next, from_prev, dim):
    count = keep.shape[dim]
    below = jnp.concatenate([lax.slice_in_dim(lower, 1, count, axis=dim), from_next], axis=dim)
    above = jnp.concatenate([from_prev, lax.slice_in_dim(upper, 0, count - 1, axis=dim)], axis=dim)
    return keep + below + above


def back_depth(grad, code):
    keep, lower, upper = split_grad(grad, code)
    count = grad.shape[0]
    from_next = passed_along(lower[0:1], "gz", -1)
    from_prev = passed_along(upper[count - 1 : count], "gz", 1)
    return join_grad(keep, lower, upper, from_next, from_prev, 0)


def back_rows(grad, code):
    keep, lower, upper = split_grad(grad, code)
    count = grad.shape[1]
    from_next = passed_along(lower[:, 0:1], "gx", -1)
    from_prev = passed_along(upper[:, count - 1 : count], "gx", 1)
    return join_grad(keep, lower, upper, from_next, from_prev, 1)


def back_columns(grad, code):
    keep, lower, upper = split_grad(grad, code)
    count = grad.shape[2]
    from_next = passed_along(lower[:, :, 0:1], "gy", -1)
    from_prev = passed_along(upper[:, :, count - 1 : count], "gy", 1)
    return join_grad(keep, lower, upper, from_next, from_prev, 2)


def erode_back(grad, codes):
    zeros = jnp.zeros_like(grad)
    select = codes[3]
    total = back_depth(jnp.where(select == 0, grad, zeros), codes[0])
    total = total + back_rows(jnp.where(select == 1, grad, zeros), codes[1])
    return total + back_columns(jnp.where(select == 2, grad, zeros), codes[2])


def dilate_back(grad, codes):
    grad = back_columns(grad, codes[2])
    grad = back_rows(grad, codes[1])
    return back_depth(grad, codes[0])


def local(prediction, label):
    fields = jnp.stack([prediction, label])
    records = []
    current = fields
    skel = None
    for level in range(ITERS + 1):
        eroded, erode_codes = erode(current)
        opened, dilate_codes = dilate(eroded)
        before = current - opened
        delta = jnp.where(before > 0, before, jnp.zeros_like(before))
        if level == 0:
            skel = delta
            records.append(
                (
                    tuple((c[0] for c in erode_codes)),
                    tuple((c[0] for c in dilate_codes)),
                    before[0],
                    delta[0],
                    None,
                    None,
                )
            )
        else:
            inside = delta - skel * delta
            records.append(
                (
                    tuple((c[0] for c in erode_codes)),
                    tuple((c[0] for c in dilate_codes)),
                    before[0],
                    delta[0],
                    inside[0],
                    skel[0],
                )
            )
            skel = skel + jnp.where(inside > 0, inside, jnp.zeros_like(inside))
        current = eroded
    pred_skel = skel[0]
    label_skel = skel[1]
    intersection, pred_total, cover, label_total = lax.psum(
        (
            jnp.sum(pred_skel * label),
            jnp.sum(pred_skel),
            jnp.sum(label_skel * prediction),
            jnp.sum(label_skel),
        ),
        ("gz", "gx", "gy"),
    )
    tprec = (intersection + 1.0) / (pred_total + 1.0)
    tsens = (cover + 1.0) / (label_total + 1.0)
    loss = 1.0 - 2.0 * tprec * tsens / (tprec + tsens)
    square = (tprec + tsens) * (tprec + tsens)
    by_prec = -2.0 * tsens * tsens / square
    by_sens = -2.0 * tprec * tprec / square
    grad_skel = by_prec * (label - tprec) / (pred_total + 1.0)
    direct = by_sens * label_skel / (label_total + 1.0)
    grad_deltas = [None] * (ITERS + 1)
    for level in range(ITERS, 0, -1):
        inside = records[level][4]
        prior = records[level][5]
        delta = records[level][3]
        grad_inside = jnp.where(inside > 0, grad_skel, jnp.zeros_like(grad_skel))
        grad_deltas[level] = grad_inside * (1.0 - prior)
        grad_skel = grad_skel - grad_inside * delta
    grad_deltas[0] = grad_skel
    grad_next = jnp.zeros_like(prediction)
    for level in range(ITERS, -1, -1):
        erode_codes, dilate_codes, before, delta, inside, prior = records[level]
        grad_before = jnp.where(before > 0, grad_deltas[level], jnp.zeros_like(before))
        grad_next = grad_next + dilate_back(-grad_before, dilate_codes)
        grad_next = grad_before + erode_back(grad_next, erode_codes)
    voxels = (
        prediction.shape[0]
        * prediction.shape[1]
        * prediction.shape[2]
        * lax.axis_size("gz")
        * lax.axis_size("gx")
        * lax.axis_size("gy")
    )
    return (loss, (grad_next + direct) * voxels)


def solution(mesh):
    in_specs = (P("gz", "gx", "gy"), P("gz", "gx", "gy"))
    out_specs = (P(), P("gz", "gx", "gy"))
    return jax.shard_map(local, mesh=mesh, in_specs=in_specs, out_specs=out_specs, check_vma=False)
```

profile of v0, /device:TPU:32, one launch (start us, length us, event | category | flops | bytes accessed | tf_op | source)
XLA Modules:
  0.0 716.4 jit_solution(103449628743789603)
XLA Ops:
  7.3 4.9 collective-permute-start.2
  12.3 5.4 collective-permute-start.3
  23.1 4.5 collective-permute-start.4
  38.9 4.3 collective-permute-start.12
  43.3 6.0 collective-permute-start.13
  51.4 8.4 %collective-permute-start.8 = (f32[2,32,1,128]{3,2,1,0:T(1,128)S(1)}, f32[2,32,1,128]{3,2,1,0:T(1,128)S(1)}, u32[]{:S(2)}, u32[]{:S(2)}) collective-permute-start(f32[2,32,1,128]{3,2,1,0:T(1,128)S(1)} %get-tuple-element.304), channel_id=1, source_target_pairs={{2,0},{4,2},{6,4},{8,6},{10,8},{12,10},{14,12},{16,14},{18,16},{20... | collective-permute-start | bytes 98312 | tf_op jit(solution)/shard_map/ppermute | solution.py:17
  64.0 6.2 collective-permute-start.11
  75.5 5.1 collective-permute-start.14
  98.1 8.1 %collective-permute-start.23 = (f32[2,34,1,128]{3,2,1,0:T(1,128)S(1)}, f32[2,34,1,128]{3,2,1,0:T(1,128)S(1)}, u32[]{:S(2)}, u32[]{:S(2)}) collective-permute-start(f32[2,34,1,128]{3,2,1,0:T(1,128)S(1)} %get-tuple-element.261), channel_id=1, source_target_pairs={{2,0},{4,2},{6,4},{8,6},{10,8},{12,10},{14,12},{16,14},{18,16},{20... | collective-permute-start | bytes 104456 | tf_op jit(solution)/shard_map/ppermute | solution.py:17
  108.3 8.6 %collective-permute-start.18 = (f32[2,32,1,128]{3,2,1,0:T(1,128)S(1)}, f32[2,32,1,128]{3,2,1,0:T(1,128)S(1)}, u32[]{:S(2)}, u32[]{:S(2)}) collective-permute-start(f32[2,32,1,128]{3,2,1,0:T(1,128)S(1)} %get-tuple-element.300), channel_id=1, source_target_pairs={{2,0},{4,2},{6,4},{8,6},{10,8},{12,10},{14,12},{16,14},{18,16},{20... | collective-permute-start | bytes 98312 | tf_op jit(solution)/shard_map/ppermute | solution.py:17
  124.5 4.5 collective-permute-start.24
  131.4 6.2 collective-permute-start.21
  154.9 8.7 %collective-permute-start.28 = (f32[2,32,1,128]{3,2,1,0:T(1,128)S(1)}, f32[2,32,1,128]{3,2,1,0:T(1,128)S(1)}, u32[]{:S(2)}, u32[]{:S(2)}) collective-permute-start(f32[2,32,1,128]{3,2,1,0:T(1,128)S(1)} %get-tuple-element.308), channel_id=1, source_target_pairs={{2,0},{4,2},{6,4},{8,6},{10,8},{12,10},{14,12},{16,14},{18,16},{20... | collective-permute-start | bytes 98312 | tf_op jit(solution)/shard_map/ppermute | solution.py:17
  164.5 5.4 collective-permute-start.33
  173.5 6.2 collective-permute-start.31
  186.2 5.7 collective-permute-start.34
  191.9 3.8 multiply_subtract_fusion.3
  208.8 3.2 fusion.24
  214.0 8.4 %collective-permute-start.43 = (f32[2,34,1,128]{3,2,1,0:T(1,128)S(1)}, f32[2,34,1,128]{3,2,1,0:T(1,128)S(1)}, u32[]{:S(2)}, u32[]{:S(2)}) collective-permute-start(f32[2,34,1,128]{3,2,1,0:T(1,128)S(1)} %get-tuple-element.257), channel_id=1, source_target_pairs={{2,0},{4,2},{6,4},{8,6},{10,8},{12,10},{14,12},{16,14},{18,16},{20... | collective-permute-start | bytes 104456 | tf_op jit(solution)/shard_map/ppermute | solution.py:17
  224.5 8.4 %collective-permute-start.38 = (f32[2,32,1,128]{3,2,1,0:T(1,128)S(1)}, f32[2,32,1,128]{3,2,1,0:T(1,128)S(1)}, u32[]{:S(2)}, u32[]{:S(2)}) collective-permute-start(f32[2,32,1,128]{3,2,1,0:T(1,128)S(1)} %get-tuple-element.312), channel_id=1, source_target_pairs={{2,0},{4,2},{6,4},{8,6},{10,8},{12,10},{14,12},{16,14},{18,16},{20... | collective-permute-start | bytes 98312 | tf_op jit(solution)/shard_map/ppermute | solution.py:17
  240.6 4.5 collective-permute-start.44
  247.6 6.1 collective-permute-start.41
  270.9 8.7 %collective-permute-start.48 = (f32[2,32,1,128]{3,2,1,0:T(1,128)S(1)}, f32[2,32,1,128]{3,2,1,0:T(1,128)S(1)}, u32[]{:S(2)}, u32[]{:S(2)}) collective-permute-start(f32[2,32,1,128]{3,2,1,0:T(1,128)S(1)} %get-tuple-element.316), channel_id=1, source_target_pairs={{2,0},{4,2},{6,4},{8,6},{10,8},{12,10},{14,12},{16,14},{18,16},{20... | collective-permute-start | bytes 98312 | tf_op jit(solution)/shard_map/ppermute | solution.py:17
  280.6 5.4 collective-permute-start.53
  289.7 6.1 collective-permute-start.51
  302.3 5.9 collective-permute-start.54
  308.2 4.1 multiply_subtract_fusion.1
  326.9 3.2 fusion.12
  332.1 8.4 %collective-permute-start.58 = (f32[2,32,1,128]{3,2,1,0:T(1,128)S(1)}, f32[2,32,1,128]{3,2,1,0:T(1,128)S(1)}, u32[]{:S(2)}, u32[]{:S(2)}) collective-permute-start(f32[2,32,1,128]{3,2,1,0:T(1,128)S(1)} %get-tuple-element.320), channel_id=1, source_target_pairs={{2,0},{4,2},{6,4},{8,6},{10,8},{12,10},{14,12},{16,14},{18,16},{20... | collective-permute-start | bytes 98312 | tf_op jit(solution)/shard_map/ppermute | solution.py:17
  344.1 4.6 collective-permute-start.61
  349.6 8.8 %collective-permute-done.60 = f32[2,32,16,1]{3,2,1,0:T(8,128)S(1)} collective-permute-done((f32[2,32,16,1]{3,2,1,0:T(8,128)S(1)}, f32[2,32,16,1]{3,2,1,0:T(8,128)S(1)}, u32[]{:S(2)}, u32[]{:S(2)}) %collective-permute-start.60) | collective-permute-done | bytes 4128 | tf_op jit(solution)/shard_map/ppermute | solution.py:17
  363.5 68.5 %all-reduce = (f32[]{:T(128)}, f32[]{:T(128)}, f32[]{:T(128)}, f32[]{:T(128)}) all-reduce(f32[]{:T(128)} %get-tuple-element.7, f32[]{:T(128)} %get-tuple-element.5, f32[]{:T(128)} %get-tuple-element.6, f32[]{:T(128)} %get-tuple-element.4), channel_id=1, replica_groups=mesh['gz'=2,'gx'=32,'gy'=2] {'gz','gx','gy'}, use_global_device_ids=true, to_apply=%region_1.2 | all-reduce | flops 4 | bytes 32 | tf_op jit(solution)/shard_map/psum | solution.py:174
  446.6 4.8 collective-permute-start.123
  457.9 4.4 collective-permute-start.75
  467.4 8.0 %collective-permute-done.110 = f32[32,16,1]{2,1,0:T(8,128)S(1)} collective-permute-done((f32[32,16,1]{2,1,0:T(8,128)S(1)}, f32[32,16,1]{2,1,0:T(8,128)S(1)}, u32[]{:S(2)}, u32[]{:S(2)}) %collective-permute-start.110) | collective-permute-done | bytes 2080 | tf_op jit(solution)/shard_map/ppermute | solution.py:25
  481.0 4.6 collective-permute-start.65
  486.0 5.8 collective-permute-start.64
  494.9 8.3 %collective-permute-start.124 = (f32[32,1,128]{2,1,0:T(1,128)S(1)}, f32[32,1,128]{2,1,0:T(1,128)S(1)}, u32[]{:S(2)}, u32[]{:S(2)}) collective-permute-start(f32[32,1,128]{2,1,0:T(1,128)S(1)} %slice.1848), channel_id=1, source_target_pairs={{2,0},{4,2},{6,4},{8,6},{10,8},{12,10},{14,12},{16,14},{18,16},{20... | collective-permute-start | bytes 49160 | tf_op jit(solution)/shard_map/ppermute | solution.py:25
  505.4 8.4 %collective-permute-start.112 = (f32[32,1,128]{2,1,0:T(1,128)S(1)}, f32[32,1,128]{2,1,0:T(1,128)S(1)}, u32[]{:S(2)}, u32[]{:S(2)}) collective-permute-start(f32[32,1,128]{2,1,0:T(1,128)S(1)} %slice.1814), channel_id=1, source_target_pairs={{2,0},{4,2},{6,4},{8,6},{10,8},{12,10},{14,12},{16,14},{18,16},{20... | collective-permute-start | bytes 49160 | tf_op jit(solution)/shard_map/ppermute | solution.py:25
  516.1 8.6 %collective-permute-start.100 = (f32[32,1,128]{2,1,0:T(1,128)S(1)}, f32[32,1,128]{2,1,0:T(1,128)S(1)}, u32[]{:S(2)}, u32[]{:S(2)}) collective-permute-start(f32[32,1,128]{2,1,0:T(1,128)S(1)} %slice.1780), channel_id=1, source_target_pairs={{2,0},{4,2},{6,4},{8,6},{10,8},{12,10},{14,12},{16,14},{18,16},{20... | collective-permute-start | bytes 49160 | tf_op jit(solution)/shard_map/ppermute | solution.py:25
  528.8 8.4 %collective-permute-start.76 = (f32[32,1,128]{2,1,0:T(1,128)S(1)}, f32[32,1,128]{2,1,0:T(1,128)S(1)}, u32[]{:S(2)}, u32[]{:S(2)}) collective-permute-start(f32[32,1,128]{2,1,0:T(1,128)S(1)} %slice.1712), channel_id=1, source_target_pairs={{2,0},{4,2},{6,4},{8,6},{10,8},{12,10},{14,12},{16,14},{18,16},{20... | collective-permute-start | bytes 49160 | tf_op jit(solution)/shard_map/ppermute | solution.py:25
  537.5 5.4 collective-permute-start.88
  545.9 3.0 collective-permute-start.79
  559.5 5.0 collective-permute-start.70
  571.2 3.5 collective-permute-done.71
  575.9 3.7 collective-permute-start.85
  584.2 6.3 collective-permute-start.82
  592.9 2.9 collective-permute-start.103
  597.1 3.6 collective-permute-done.83
  601.9 3.7 collective-permute-start.97
  610.2 6.3 collective-permute-start.94
  619.2 2.9 collective-permute-start.115
  623.4 3.4 collective-permute-done.95
  628.0 3.7 collective-permute-start.109
  636.3 6.6 collective-permute-start.106
  645.2 2.9 collective-permute-start.127
  649.4 3.6 collective-permute-done.107
  654.1 3.7 collective-permute-start.121
  661.1 6.3 collective-permute-start.118
  671.2 9.4 %collective-permute-done.120 = f32[32,16,1]{2,1,0:T(8,128)S(1)} collective-permute-done((f32[32,16,1]{2,1,0:T(8,128)S(1)}, f32[32,16,1]{2,1,0:T(8,128)S(1)}, u32[]{:S(2)}, u32[]{:S(2)}) %collective-permute-start.120) | collective-permute-done | bytes 2080 | tf_op jit(solution)/shard_map/ppermute | solution.py:25
  681.8 8.2 %collective-permute-start.130 = (f32[32,1,128]{2,1,0:T(1,128)S(1)}, f32[32,1,128]{2,1,0:T(1,128)S(1)}, u32[]{:S(2)}, u32[]{:S(2)}) collective-permute-start(f32[32,1,128]{2,1,0:T(1,128)S(1)} %slice.1862), channel_id=1, source_target_pairs={{2,0},{4,2},{6,4},{8,6},{10,8},{12,10},{14,12},{16,14},{18,16},{20... | collective-permute-start | bytes 49160 | tf_op jit(solution)/shard_map/ppermute | solution.py:25
  693.5 3.0 collective-permute-start.129
  698.0 5.4 collective-permute-done.133
  705.0 7.5 %collective-permute-done.132 = f32[32,16,1]{2,1,0:T(8,128)} collective-permute-done((f32[32,16,1]{2,1,0:T(8,128)S(1)}, f32[32,16,1]{2,1,0:T(8,128)}, u32[]{:S(2)}, u32[]{:S(2)}) %collective-permute-start.132) | collective-permute-done | bytes 2080 | tf_op jit(solution)/shard_map/ppermute | solution.py:25
  (744 shorter events, 279.0 us)
Async XLA Ops:
  38.9 32.3 %collective-permute-start.12 = (f32[2,34,1,128]{3,2,1,0:T(1,128)S(1)}, f32[2,34,1,128]{3,2,1,0:T(1,128)S(1)}, u32[]{:S(2)}, u32[]{:S(2)}) collective-permute-start(f32[2,34,1,128]{3,2,1,0:T(1,128)S(1)} %get-tuple-element.262), channel_id=1, source_target_pairs={{0,2},{2,4},{4,6},{6,8},{8,10},{10,12},{12,14},{14,16},{16,18},{18... | collective-permute-start | bytes 104456 | tf_op jit(solution)/shard_map/ppermute | solution.py:16
  43.3 27.9 %collective-permute-start.13 = (f32[2,34,1,128]{3,2,1,0:T(1,128)S(1)}, f32[2,34,1,128]{3,2,1,0:T(1,128)S(1)}, u32[]{:S(2)}, u32[]{:S(2)}) collective-permute-start(f32[2,34,1,128]{3,2,1,0:T(1,128)S(1)} %get-tuple-element.263), channel_id=1, source_target_pairs={{2,0},{4,2},{6,4},{8,6},{10,8},{12,10},{14,12},{16,14},{18,16},{20... | collective-permute-start | bytes 104456 | tf_op jit(solution)/shard_map/ppermute | solution.py:17
  62.7 17.9 %collective-permute-start.10 = (f32[2,32,16,1]{3,2,1,0:T(8,128)}, f32[2,32,16,1]{3,2,1,0:T(8,128)}, u32[]{:S(2)}, u32[]{:S(2)}) collective-permute-start(f32[2,32,16,1]{3,2,1,0:T(8,128)} %get-tuple-element.301), channel_id=1, source_target_pairs={{1,0},{3,2},{5,4},{7,6},{9,8},{11,10},{13,12},{15,14},{17,16},{19,... | collective-permute-start | bytes 12296 | tf_op jit(solution)/shard_map/ppermute | solution.py:17
  64.0 16.6 %collective-permute-start.11 = (f32[2,32,16,1]{3,2,1,0:T(8,128)}, f32[2,32,16,1]{3,2,1,0:T(8,128)}, u32[]{:S(2)}, u32[]{:S(2)}) collective-permute-start(f32[2,32,16,1]{3,2,1,0:T(8,128)} %get-tuple-element.302), channel_id=1, source_target_pairs={{0,1},{2,3},{4,5},{6,7},{8,9},{10,11},{12,13},{14,15},{16,17},{18,... | collective-permute-start | bytes 12296 | tf_op jit(solution)/shard_map/ppermute | solution.py:16
  95.3 23.2 %collective-permute-start.22 = (f32[2,34,1,128]{3,2,1,0:T(1,128)S(1)}, f32[2,34,1,128]{3,2,1,0:T(1,128)S(1)}, u32[]{:S(2)}, u32[]{:S(2)}) collective-permute-start(f32[2,34,1,128]{3,2,1,0:T(1,128)S(1)} %get-tuple-element.260), channel_id=1, source_target_pairs={{0,2},{2,4},{4,6},{6,8},{8,10},{10,12},{12,14},{14,16},{16,18},{18... | collective-permute-start | bytes 104456 | tf_op jit(solution)/shard_map/ppermute | solution.py:16
  98.1 20.4 %collective-permute-start.23 = (f32[2,34,1,128]{3,2,1,0:T(1,128)S(1)}, f32[2,34,1,128]{3,2,1,0:T(1,128)S(1)}, u32[]{:S(2)}, u32[]{:S(2)}) collective-permute-start(f32[2,34,1,128]{3,2,1,0:T(1,128)S(1)} %get-tuple-element.261), channel_id=1, source_target_pairs={{2,0},{4,2},{6,4},{8,6},{10,8},{12,10},{14,12},{16,14},{18,16},{20... | collective-permute-start | bytes 104456 | tf_op jit(solution)/shard_map/ppermute | solution.py:17
  123.2 15.8 %collective-permute-start.25 = (f32[2,34,18,1]{1,0,3,2:T(2,128)S(1)}, f32[2,34,18,1]{1,0,3,2:T(2,128)S(1)}, u32[]{:S(2)}, u32[]{:S(2)}) collective-permute-start(f32[2,34,18,1]{1,0,3,2:T(2,128)S(1)} %copy.73), channel_id=1, source_target_pairs={{1,0},{3,2},{5,4},{7,6},{9,8},{11,10},{13,12},{15,14},{17,16},{19,... | collective-permute-start | bytes 14696 | tf_op jit(solution)/shard_map/ppermute | solution.py:17
  130.2 56.0 %collective-permute-start.20 = (f32[2,32,16,1]{3,2,1,0:T(8,128)}, f32[2,32,16,1]{3,2,1,0:T(8,128)}, u32[]{:S(2)}, u32[]{:S(2)}) collective-permute-start(f32[2,32,16,1]{3,2,1,0:T(8,128)} %get-tuple-element.297), channel_id=1, source_target_pairs={{1,0},{3,2},{5,4},{7,6},{9,8},{11,10},{13,12},{15,14},{17,16},{19,... | collective-permute-start | bytes 12296 | tf_op jit(solution)/shard_map/ppermute | solution.py:17
  131.4 60.4 %collective-permute-start.21 = (f32[2,32,16,1]{3,2,1,0:T(8,128)}, f32[2,32,16,1]{3,2,1,0:T(8,128)}, u32[]{:S(2)}, u32[]{:S(2)}) collective-permute-start(f32[2,32,16,1]{3,2,1,0:T(8,128)} %get-tuple-element.298), channel_id=1, source_target_pairs={{0,1},{2,3},{4,5},{6,7},{8,9},{10,11},{12,13},{14,15},{16,17},{18,... | collective-permute-start | bytes 12296 | tf_op jit(solution)/shard_map/ppermute | solution.py:16
  150.9 22.6 %collective-permute-start.32 = (f32[2,34,1,128]{3,2,1,0:T(1,128)S(1)}, f32[2,34,1,128]{3,2,1,0:T(1,128)S(1)}, u32[]{:S(2)}, u32[]{:S(2)}) collective-permute-start(f32[2,34,1,128]{3,2,1,0:T(1,128)S(1)} %get-tuple-element.258), channel_id=1, source_target_pairs={{0,2},{2,4},{4,6},{6,8},{8,10},{10,12},{12,14},{14,16},{16,18},{18... | collective-permute-start | bytes 104456 | tf_op jit(solution)/shard_map/ppermute | solution.py:16
  154.9 15.0 %collective-permute-start.28 = (f32[2,32,1,128]{3,2,1,0:T(1,128)S(1)}, f32[2,32,1,128]{3,2,1,0:T(1,128)S(1)}, u32[]{:S(2)}, u32[]{:S(2)}) collective-permute-start(f32[2,32,1,128]{3,2,1,0:T(1,128)S(1)} %get-tuple-element.308), channel_id=1, source_target_pairs={{2,0},{4,2},{6,4},{8,6},{10,8},{12,10},{14,12},{16,14},{18,16},{20... | collective-permute-start | bytes 98312 | tf_op jit(solution)/shard_map/ppermute | solution.py:17
  164.5 15.2 %collective-permute-start.33 = (f32[2,34,1,128]{3,2,1,0:T(1,128)S(1)}, f32[2,34,1,128]{3,2,1,0:T(1,128)S(1)}, u32[]{:S(2)}, u32[]{:S(2)}) collective-permute-start(f32[2,34,1,128]{3,2,1,0:T(1,128)S(1)} %get-tuple-element.259), channel_id=1, source_target_pairs={{2,0},{4,2},{6,4},{8,6},{10,8},{12,10},{14,12},{16,14},{18,16},{20... | collective-permute-start | bytes 104456 | tf_op jit(solution)/shard_map/ppermute | solution.py:17
  171.3 20.6 %collective-permute-start.30 = (f32[2,32,16,1]{3,2,1,0:T(8,128)}, f32[2,32,16,1]{3,2,1,0:T(8,128)}, u32[]{:S(2)}, u32[]{:S(2)}) collective-permute-start(f32[2,32,16,1]{3,2,1,0:T(8,128)} %get-tuple-element.305), channel_id=1, source_target_pairs={{1,0},{3,2},{5,4},{7,6},{9,8},{11,10},{13,12},{15,14},{17,16},{19,... | collective-permute-start | bytes 12296 | tf_op jit(solution)/shard_map/ppermute | solution.py:17
  173.5 18.4 %collective-permute-start.31 = (f32[2,32,16,1]{3,2,1,0:T(8,128)}, f32[2,32,16,1]{3,2,1,0:T(8,128)}, u32[]{:S(2)}, u32[]{:S(2)}) collective-permute-start(f32[2,32,16,1]{3,2,1,0:T(8,128)} %get-tuple-element.306), channel_id=1, source_target_pairs={{0,1},{2,3},{4,5},{6,7},{8,9},{10,11},{12,13},{14,15},{16,17},{18,... | collective-permute-start | bytes 12296 | tf_op jit(solution)/shard_map/ppermute | solution.py:16
  212.1 22.7 %collective-permute-start.42 = (f32[2,34,1,128]{3,2,1,0:T(1,128)S(1)}, f32[2,34,1,128]{3,2,1,0:T(1,128)S(1)}, u32[]{:S(2)}, u32[]{:S(2)}) collective-permute-start(f32[2,34,1,128]{3,2,1,0:T(1,128)S(1)} %get-tuple-element.256), channel_id=1, source_target_pairs={{0,2},{2,4},{4,6},{6,8},{8,10},{10,12},{12,14},{14,16},{16,18},{18... | collective-permute-start | bytes 104456 | tf_op jit(solution)/shard_map/ppermute | solution.py:16
  214.0 20.7 %collective-permute-start.43 = (f32[2,34,1,128]{3,2,1,0:T(1,128)S(1)}, f32[2,34,1,128]{3,2,1,0:T(1,128)S(1)}, u32[]{:S(2)}, u32[]{:S(2)}) collective-permute-start(f32[2,34,1,128]{3,2,1,0:T(1,128)S(1)} %get-tuple-element.257), channel_id=1, source_target_pairs={{2,0},{4,2},{6,4},{8,6},{10,8},{12,10},{14,12},{16,14},{18,16},{20... | collective-permute-start | bytes 104456 | tf_op jit(solution)/shard_map/ppermute | solution.py:17
  239.3 15.8 %collective-permute-start.45 = (f32[2,34,18,1]{1,0,3,2:T(2,128)S(1)}, f32[2,34,18,1]{1,0,3,2:T(2,128)S(1)}, u32[]{:S(2)}, u32[]{:S(2)}) collective-permute-start(f32[2,34,18,1]{1,0,3,2:T(2,128)S(1)} %copy.81), channel_id=1, source_target_pairs={{1,0},{3,2},{5,4},{7,6},{9,8},{11,10},{13,12},{15,14},{17,16},{19,... | collective-permute-start | bytes 14696 | tf_op jit(solution)/shard_map/ppermute | solution.py:17
  246.3 56.0 %collective-permute-start.40 = (f32[2,32,16,1]{3,2,1,0:T(8,128)}, f32[2,32,16,1]{3,2,1,0:T(8,128)}, u32[]{:S(2)}, u32[]{:S(2)}) collective-permute-start(f32[2,32,16,1]{3,2,1,0:T(8,128)} %get-tuple-element.309), channel_id=1, source_target_pairs={{1,0},{3,2},{5,4},{7,6},{9,8},{11,10},{13,12},{15,14},{17,16},{19,... | collective-permute-start | bytes 12296 | tf_op jit(solution)/shard_map/ppermute | solution.py:17
  247.6 60.6 %collective-permute-start.41 = (f32[2,32,16,1]{3,2,1,0:T(8,128)}, f32[2,32,16,1]{3,2,1,0:T(8,128)}, u32[]{:S(2)}, u32[]{:S(2)}) collective-permute-start(f32[2,32,16,1]{3,2,1,0:T(8,128)} %get-tuple-element.310), channel_id=1, source_target_pairs={{0,1},{2,3},{4,5},{6,7},{8,9},{10,11},{12,13},{14,15},{16,17},{18,... | collective-permute-start | bytes 12296 | tf_op jit(solution)/shard_map/ppermute | solution.py:16
  266.9 22.8 %collective-permute-start.52 = (f32[2,34,1,128]{3,2,1,0:T(1,128)S(1)}, f32[2,34,1,128]{3,2,1,0:T(1,128)S(1)}, u32[]{:S(2)}, u32[]{:S(2)}) collective-permute-start(f32[2,34,1,128]{3,2,1,0:T(1,128)S(1)} %get-tuple-element.254), channel_id=1, source_target_pairs={{0,2},{2,4},{4,6},{6,8},{8,10},{10,12},{12,14},{14,16},{16,18},{18... | collective-permute-start | bytes 104456 | tf_op jit(solution)/shard_map/ppermute | solution.py:16
  270.9 15.0 %collective-permute-start.48 = (f32[2,32,1,128]{3,2,1,0:T(1,128)S(1)}, f32[2,32,1,128]{3,2,1,0:T(1,128)S(1)}, u32[]{:S(2)}, u32[]{:S(2)}) collective-permute-start(f32[2,32,1,128]{3,2,1,0:T(1,128)S(1)} %get-tuple-element.316), channel_id=1, source_target_pairs={{2,0},{4,2},{6,4},{8,6},{10,8},{12,10},{14,12},{16,14},{18,16},{20... | collective-permute-start | bytes 98312 | tf_op jit(solution)/shard_map/ppermute | solution.py:17
  280.6 15.3 %collective-permute-start.53 = (f32[2,34,1,128]{3,2,1,0:T(1,128)S(1)}, f32[2,34,1,128]{3,2,1,0:T(1,128)S(1)}, u32[]{:S(2)}, u32[]{:S(2)}) collective-permute-start(f32[2,34,1,128]{3,2,1,0:T(1,128)S(1)} %get-tuple-element.255), channel_id=1, source_target_pairs={{2,0},{4,2},{6,4},{8,6},{10,8},{12,10},{14,12},{16,14},{18,16},{20... | collective-permute-start | bytes 104456 | tf_op jit(solution)/shard_map/ppermute | solution.py:17
  287.4 20.7 %collective-permute-start.50 = (f32[2,32,16,1]{3,2,1,0:T(8,128)}, f32[2,32,16,1]{3,2,1,0:T(8,128)}, u32[]{:S(2)}, u32[]{:S(2)}) collective-permute-start(f32[2,32,16,1]{3,2,1,0:T(8,128)} %get-tuple-element.313), channel_id=1, source_target_pairs={{1,0},{3,2},{5,4},{7,6},{9,8},{11,10},{13,12},{15,14},{17,16},{19,... | collective-permute-start | bytes 12296 | tf_op jit(solution)/shard_map/ppermute | solution.py:17
  289.7 18.5 %collective-permute-start.51 = (f32[2,32,16,1]{3,2,1,0:T(8,128)}, f32[2,32,16,1]{3,2,1,0:T(8,128)}, u32[]{:S(2)}, u32[]{:S(2)}) collective-permute-start(f32[2,32,16,1]{3,2,1,0:T(8,128)} %get-tuple-element.314), channel_id=1, source_target_pairs={{0,1},{2,3},{4,5},{6,7},{8,9},{10,11},{12,13},{14,15},{16,17},{18,... | collective-permute-start | bytes 12296 | tf_op jit(solution)/shard_map/ppermute | solution.py:16
  301.0 15.3 %collective-permute-start.55 = (f32[2,34,18,1]{1,0,3,2:T(2,128)S(1)}, f32[2,34,18,1]{1,0,3,2:T(2,128)}, u32[]{:S(2)}, u32[]{:S(2)}) collective-permute-start(f32[2,34,18,1]{1,0,3,2:T(2,128)S(1)} %copy.85), channel_id=1, source_target_pairs={{1,0},{3,2},{5,4},{7,6},{9,8},{11,10},{13,12},{15,14},{17,16},{19,... | collective-permute-start | bytes 14696 | tf_op jit(solution)/shard_map/ppermute | solution.py:17
  342.6 15.8 %collective-permute-start.60 = (f32[2,32,16,1]{3,2,1,0:T(8,128)S(1)}, f32[2,32,16,1]{3,2,1,0:T(8,128)S(1)}, u32[]{:S(2)}, u32[]{:S(2)}) collective-permute-start(f32[2,32,16,1]{3,2,1,0:T(8,128)S(1)} %get-tuple-element.317), channel_id=1, source_target_pairs={{1,0},{3,2},{5,4},{7,6},{9,8},{11,10},{13,12},{15,14},{17,16},{19,... | collective-permute-start | bytes 12296 | tf_op jit(solution)/shard_map/ppermute | solution.py:17
  344.1 15.6 %collective-permute-start.61 = (f32[2,32,16,1]{3,2,1,0:T(8,128)S(1)}, f32[2,32,16,1]{3,2,1,0:T(8,128)S(1)}, u32[]{:S(2)}, u32[]{:S(2)}) collective-permute-start(f32[2,32,16,1]{3,2,1,0:T(8,128)S(1)} %get-tuple-element.318), channel_id=1, source_target_pairs={{0,1},{2,3},{4,5},{6,7},{8,9},{10,11},{12,13},{14,15},{16,17},{18,... | collective-permute-start | bytes 12296 | tf_op jit(solution)/shard_map/ppermute | solution.py:16
  451.4 14.5 %collective-permute-start.111 = (f32[32,16,1]{2,1,0:T(8,128)S(1)}, f32[32,16,1]{2,1,0:T(8,128)S(1)}, u32[]{:S(2)}, u32[]{:S(2)}) collective-permute-start(f32[32,16,1]{2,1,0:T(8,128)S(1)} %slice.1811), channel_id=1, source_target_pairs={{0,1},{2,3},{4,5},{6,7},{8,9},{10,11},{12,13},{14,15},{16,17},{18,... | collective-permute-start | bytes 6152 | tf_op jit(solution)/shard_map/ppermute | solution.py:25
  452.7 24.3 %collective-permute-start.99 = (f32[32,16,1]{2,1,0:T(8,128)S(1)}, f32[32,16,1]{2,1,0:T(8,128)S(1)}, u32[]{:S(2)}, u32[]{:S(2)}) collective-permute-start(f32[32,16,1]{2,1,0:T(8,128)S(1)} %slice.1777), channel_id=1, source_target_pairs={{0,1},{2,3},{4,5},{6,7},{8,9},{10,11},{12,13},{14,15},{16,17},{18,... | collective-permute-start | bytes 6152 | tf_op jit(solution)/shard_map/ppermute | solution.py:25
  454.1 31.9 %collective-permute-start.87 = (f32[32,16,1]{2,1,0:T(8,128)S(1)}, f32[32,16,1]{2,1,0:T(8,128)S(1)}, u32[]{:S(2)}, u32[]{:S(2)}) collective-permute-start(f32[32,16,1]{2,1,0:T(8,128)S(1)} %slice.1743), channel_id=1, source_target_pairs={{0,1},{2,3},{4,5},{6,7},{8,9},{10,11},{12,13},{14,15},{16,17},{18,... | collective-permute-start | bytes 6152 | tf_op jit(solution)/shard_map/ppermute | solution.py:25
  457.9 34.2 %collective-permute-start.75 = (f32[32,16,1]{2,1,0:T(8,128)S(1)}, f32[32,16,1]{2,1,0:T(8,128)S(1)}, u32[]{:S(2)}, u32[]{:S(2)}) collective-permute-start(f32[32,16,1]{2,1,0:T(8,128)S(1)} %slice.1709), channel_id=1, source_target_pairs={{0,1},{2,3},{4,5},{6,7},{8,9},{10,11},{12,13},{14,15},{16,17},{18,... | collective-permute-start | bytes 6152 | tf_op jit(solution)/shard_map/ppermute | solution.py:25
  465.9 15.1 %collective-permute-start.98 = (f32[32,16,1]{2,1,0:T(8,128)S(1)}, f32[32,16,1]{2,1,0:T(8,128)S(1)}, u32[]{:S(2)}, u32[]{:S(2)}) collective-permute-start(f32[32,16,1]{2,1,0:T(8,128)S(1)} %bitcast.924), channel_id=1, source_target_pairs={{1,0},{3,2},{5,4},{7,6},{9,8},{11,10},{13,12},{15,14},{17,16},{19,... | collective-permute-start | bytes 6152 | tf_op jit(solution)/shard_map/ppermute | solution.py:25
  475.4 16.4 %collective-permute-start.86 = (f32[32,16,1]{2,1,0:T(8,128)S(1)}, f32[32,16,1]{2,1,0:T(8,128)S(1)}, u32[]{:S(2)}, u32[]{:S(2)}) collective-permute-start(f32[32,16,1]{2,1,0:T(8,128)S(1)} %bitcast.923), channel_id=1, source_target_pairs={{1,0},{3,2},{5,4},{7,6},{9,8},{11,10},{13,12},{15,14},{17,16},{19,... | collective-permute-start | bytes 6152 | tf_op jit(solution)/shard_map/ppermute | solution.py:25
  477.1 15.1 %collective-permute-start.74 = (f32[32,16,1]{2,1,0:T(8,128)S(1)}, f32[32,16,1]{2,1,0:T(8,128)S(1)}, u32[]{:S(2)}, u32[]{:S(2)}) collective-permute-start(f32[32,16,1]{2,1,0:T(8,128)S(1)} %bitcast.922), channel_id=1, source_target_pairs={{1,0},{3,2},{5,4},{7,6},{9,8},{11,10},{13,12},{15,14},{17,16},{19,... | collective-permute-start | bytes 6152 | tf_op jit(solution)/shard_map/ppermute | solution.py:25
  481.0 24.4 %collective-permute-start.65 = (f32[32,1,128]{2,1,0:T(1,128)S(1)}, f32[32,1,128]{2,1,0:T(1,128)S(1)}, u32[]{:S(2)}, u32[]{:S(2)}) collective-permute-start(f32[32,1,128]{2,1,0:T(1,128)S(1)} %slice.1679), channel_id=1, source_target_pairs={{0,2},{2,4},{4,6},{6,8},{8,10},{10,12},{12,14},{14,16},{16,18},{18... | collective-permute-start | bytes 49160 | tf_op jit(solution)/shard_map/ppermute | solution.py:25
  486.0 27.9 %collective-permute-start.64 = (f32[32,1,128]{2,1,0:T(1,128)S(1)}, f32[32,1,128]{2,1,0:T(1,128)S(1)}, u32[]{:S(2)}, u32[]{:S(2)}) collective-permute-start(f32[32,1,128]{2,1,0:T(1,128)S(1)} %slice.1678), channel_id=1, source_target_pairs={{2,0},{4,2},{6,4},{8,6},{10,8},{12,10},{14,12},{16,14},{18,16},{20... | collective-permute-start | bytes 49160 | tf_op jit(solution)/shard_map/ppermute | solution.py:25
  492.9 23.2 %collective-permute-start.125 = (f32[32,1,128]{2,1,0:T(1,128)S(1)}, f32[32,1,128]{2,1,0:T(1,128)S(1)}, u32[]{:S(2)}, u32[]{:S(2)}) collective-permute-start(f32[32,1,128]{2,1,0:T(1,128)S(1)} %slice.1849), channel_id=1, source_target_pairs={{0,2},{2,4},{4,6},{6,8},{8,10},{10,12},{12,14},{14,16},{16,18},{18... | collective-permute-start | bytes 49160 | tf_op jit(solution)/shard_map/ppermute | solution.py:25
  494.9 29.8 %collective-permute-start.124 = (f32[32,1,128]{2,1,0:T(1,128)S(1)}, f32[32,1,128]{2,1,0:T(1,128)S(1)}, u32[]{:S(2)}, u32[]{:S(2)}) collective-permute-start(f32[32,1,128]{2,1,0:T(1,128)S(1)} %slice.1848), channel_id=1, source_target_pairs={{2,0},{4,2},{6,4},{8,6},{10,8},{12,10},{14,12},{16,14},{18,16},{20... | collective-permute-start | bytes 49160 | tf_op jit(solution)/shard_map/ppermute | solution.py:25
  503.3 23.6 %collective-permute-start.113 = (f32[32,1,128]{2,1,0:T(1,128)S(1)}, f32[32,1,128]{2,1,0:T(1,128)S(1)}, u32[]{:S(2)}, u32[]{:S(2)}) collective-permute-start(f32[32,1,128]{2,1,0:T(1,128)S(1)} %slice.1815), channel_id=1, source_target_pairs={{0,2},{2,4},{4,6},{6,8},{8,10},{10,12},{12,14},{14,16},{16,18},{18... | collective-permute-start | bytes 49160 | tf_op jit(solution)/shard_map/ppermute | solution.py:25
  505.4 23.4 %collective-permute-start.112 = (f32[32,1,128]{2,1,0:T(1,128)S(1)}, f32[32,1,128]{2,1,0:T(1,128)S(1)}, u32[]{:S(2)}, u32[]{:S(2)}) collective-permute-start(f32[32,1,128]{2,1,0:T(1,128)S(1)} %slice.1814), channel_id=1, source_target_pairs={{2,0},{4,2},{6,4},{8,6},{10,8},{12,10},{14,12},{16,14},{18,16},{20... | collective-permute-start | bytes 49160 | tf_op jit(solution)/shard_map/ppermute | solution.py:25
  513.9 30.7 %collective-permute-start.101 = (f32[32,1,128]{2,1,0:T(1,128)S(1)}, f32[32,1,128]{2,1,0:T(1,128)S(1)}, u32[]{:S(2)}, u32[]{:S(2)}) collective-permute-start(f32[32,1,128]{2,1,0:T(1,128)S(1)} %slice.1781), channel_id=1, source_target_pairs={{0,2},{2,4},{4,6},{6,8},{8,10},{10,12},{12,14},{14,16},{16,18},{18... | collective-permute-start | bytes 49160 | tf_op jit(solution)/shard_map/ppermute | solution.py:25
  516.1 29.9 %collective-permute-start.100 = (f32[32,1,128]{2,1,0:T(1,128)S(1)}, f32[32,1,128]{2,1,0:T(1,128)S(1)}, u32[]{:S(2)}, u32[]{:S(2)}) collective-permute-start(f32[32,1,128]{2,1,0:T(1,128)S(1)} %slice.1780), channel_id=1, source_target_pairs={{2,0},{4,2},{6,4},{8,6},{10,8},{12,10},{14,12},{16,14},{18,16},{20... | collective-permute-start | bytes 49160 | tf_op jit(solution)/shard_map/ppermute | solution.py:25
  524.7 24.7 %collective-permute-start.89 = (f32[32,1,128]{2,1,0:T(1,128)S(1)}, f32[32,1,128]{2,1,0:T(1,128)S(1)}, u32[]{:S(2)}, u32[]{:S(2)}) collective-permute-start(f32[32,1,128]{2,1,0:T(1,128)S(1)} %slice.1747), channel_id=1, source_target_pairs={{0,2},{2,4},{4,6},{6,8},{8,10},{10,12},{12,14},{14,16},{16,18},{18... | collective-permute-start | bytes 49160 | tf_op jit(solution)/shard_map/ppermute | solution.py:25
  555.4 14.5 %collective-permute-start.69 = (f32[1,16,128]{2,1,0:T(8,128)S(1)}, f32[1,16,128]{2,1,0:T(8,128)S(1)}, u32[]{:S(2)}, u32[]{:S(2)}) collective-permute-start(f32[1,16,128]{2,1,0:T(8,128)S(1)} %slice.1687), channel_id=1, source_target_pairs={{0,64},{1,65},{2,66},{3,67},{4,68},{5,69},{6,70},{7,71},{8,72},{9,... | collective-permute-start | bytes 24584 | tf_op jit(solution)/shard_map/ppermute | solution.py:25
  567.3 15.6 %collective-permute-start.91 = (f32[1,16,128]{2,1,0:T(8,128)S(1)}, f32[1,16,128]{2,1,0:T(8,128)S(1)}, u32[]{:S(2)}, u32[]{:S(2)}) collective-permute-start(f32[1,16,128]{2,1,0:T(8,128)S(1)} %slice.1751), channel_id=1, source_target_pairs={{0,64},{1,65},{2,66},{3,67},{4,68},{5,69},{6,70},{7,71},{8,72},{9,... | collective-permute-start | bytes 24584 | tf_op jit(solution)/shard_map/ppermute | solution.py:25
  575.9 14.6 %collective-permute-start.85 = (f32[32,16,1]{2,1,0:T(8,128)S(1)}, f32[32,16,1]{2,1,0:T(8,128)S(1)}, u32[]{:S(2)}, u32[]{:S(2)}) collective-permute-start(f32[32,16,1]{2,1,0:T(8,128)S(1)} %slice.1733), channel_id=1, source_target_pairs={{0,1},{2,3},{4,5},{6,7},{8,9},{10,11},{12,13},{14,15},{16,17},{18,... | collective-permute-start | bytes 6152 | tf_op jit(solution)/shard_map/ppermute | solution.py:25
  581.3 14.5 %collective-permute-start.81 = (f32[1,16,128]{2,1,0:T(8,128)S(1)}, f32[1,16,128]{2,1,0:T(8,128)S(1)}, u32[]{:S(2)}, u32[]{:S(2)}) collective-permute-start(f32[1,16,128]{2,1,0:T(8,128)S(1)} %slice.1721), channel_id=1, source_target_pairs={{0,64},{1,65},{2,66},{3,67},{4,68},{5,69},{6,70},{7,71},{8,72},{9,... | collective-permute-start | bytes 24584 | tf_op jit(solution)/shard_map/ppermute | solution.py:25
  592.9 16.0 %collective-permute-start.103 = (f32[1,16,128]{2,1,0:T(8,128)S(1)}, f32[1,16,128]{2,1,0:T(8,128)S(1)}, u32[]{:S(2)}, u32[]{:S(2)}) collective-permute-start(f32[1,16,128]{2,1,0:T(8,128)S(1)} %slice.1785), channel_id=1, source_target_pairs={{0,64},{1,65},{2,66},{3,67},{4,68},{5,69},{6,70},{7,71},{8,72},{9,... | collective-permute-start | bytes 24584 | tf_op jit(solution)/shard_map/ppermute | solution.py:25
  601.9 14.6 %collective-permute-start.97 = (f32[32,16,1]{2,1,0:T(8,128)S(1)}, f32[32,16,1]{2,1,0:T(8,128)S(1)}, u32[]{:S(2)}, u32[]{:S(2)}) collective-permute-start(f32[32,16,1]{2,1,0:T(8,128)S(1)} %slice.1767), channel_id=1, source_target_pairs={{0,1},{2,3},{4,5},{6,7},{8,9},{10,11},{12,13},{14,15},{16,17},{18,... | collective-permute-start | bytes 6152 | tf_op jit(solution)/shard_map/ppermute | solution.py:25
  607.3 14.8 %collective-permute-start.93 = (f32[1,16,128]{2,1,0:T(8,128)S(1)}, f32[1,16,128]{2,1,0:T(8,128)S(1)}, u32[]{:S(2)}, u32[]{:S(2)}) collective-permute-start(f32[1,16,128]{2,1,0:T(8,128)S(1)} %slice.1755), channel_id=1, source_target_pairs={{0,64},{1,65},{2,66},{3,67},{4,68},{5,69},{6,70},{7,71},{8,72},{9,... | collective-permute-start | bytes 24584 | tf_op jit(solution)/shard_map/ppermute | solution.py:25
  619.2 15.8 %collective-permute-start.115 = (f32[1,16,128]{2,1,0:T(8,128)S(1)}, f32[1,16,128]{2,1,0:T(8,128)S(1)}, u32[]{:S(2)}, u32[]{:S(2)}) collective-permute-start(f32[1,16,128]{2,1,0:T(8,128)S(1)} %slice.1819), channel_id=1, source_target_pairs={{0,64},{1,65},{2,66},{3,67},{4,68},{5,69},{6,70},{7,71},{8,72},{9,... | collective-permute-start | bytes 24584 | tf_op jit(solution)/shard_map/ppermute | solution.py:25
  628.0 14.9 %collective-permute-start.109 = (f32[32,16,1]{2,1,0:T(8,128)S(1)}, f32[32,16,1]{2,1,0:T(8,128)S(1)}, u32[]{:S(2)}, u32[]{:S(2)}) collective-permute-start(f32[32,16,1]{2,1,0:T(8,128)S(1)} %slice.1801), channel_id=1, source_target_pairs={{0,1},{2,3},{4,5},{6,7},{8,9},{10,11},{12,13},{14,15},{16,17},{18,... | collective-permute-start | bytes 6152 | tf_op jit(solution)/shard_map/ppermute | solution.py:25
  633.3 14.8 %collective-permute-start.105 = (f32[1,16,128]{2,1,0:T(8,128)S(1)}, f32[1,16,128]{2,1,0:T(8,128)S(1)}, u32[]{:S(2)}, u32[]{:S(2)}) collective-permute-start(f32[1,16,128]{2,1,0:T(8,128)S(1)} %slice.1789), channel_id=1, source_target_pairs={{0,64},{1,65},{2,66},{3,67},{4,68},{5,69},{6,70},{7,71},{8,72},{9,... | collective-permute-start | bytes 24584 | tf_op jit(solution)/shard_map/ppermute | solution.py:25
  635.0 14.4 %collective-permute-start.104 = (f32[1,16,128]{2,1,0:T(8,128)S(1)}, f32[1,16,128]{2,1,0:T(8,128)S(1)}, u32[]{:S(2)}, u32[]{:S(2)}) collective-permute-start(f32[1,16,128]{2,1,0:T(8,128)S(1)} %slice.1788), channel_id=1, source_target_pairs={{64,0},{65,1},{66,2},{67,3},{68,4},{69,5},{70,6},{71,7},{72,8},{73... | collective-permute-start | bytes 24584 | tf_op jit(solution)/shard_map/ppermute | solution.py:25
  645.2 15.9 %collective-permute-start.127 = (f32[1,16,128]{2,1,0:T(8,128)S(1)}, f32[1,16,128]{2,1,0:T(8,128)S(1)}, u32[]{:S(2)}, u32[]{:S(2)}) collective-permute-start(f32[1,16,128]{2,1,0:T(8,128)S(1)} %slice.1853), channel_id=1, source_target_pairs={{0,64},{1,65},{2,66},{3,67},{4,68},{5,69},{6,70},{7,71},{8,72},{9,... | collective-permute-start | bytes 24584 | tf_op jit(solution)/shard_map/ppermute | solution.py:25
  648.1 19.3 %collective-permute-start.126 = (f32[1,16,128]{2,1,0:T(8,128)S(1)}, f32[1,16,128]{2,1,0:T(8,128)S(1)}, u32[]{:S(2)}, u32[]{:S(2)}) collective-permute-start(f32[1,16,128]{2,1,0:T(8,128)S(1)} %slice.1852), channel_id=1, source_target_pairs={{64,0},{65,1},{66,2},{67,3},{68,4},{69,5},{70,6},{71,7},{72,8},{73... | collective-permute-start | bytes 24584 | tf_op jit(solution)/shard_map/ppermute | solution.py:25
  654.1 15.4 %collective-permute-start.121 = (f32[32,16,1]{2,1,0:T(8,128)S(1)}, f32[32,16,1]{2,1,0:T(8,128)S(1)}, u32[]{:S(2)}, u32[]{:S(2)}) collective-permute-start(f32[32,16,1]{2,1,0:T(8,128)S(1)} %slice.1835), channel_id=1, source_target_pairs={{0,1},{2,3},{4,5},{6,7},{8,9},{10,11},{12,13},{14,15},{16,17},{18,... | collective-permute-start | bytes 6152 | tf_op jit(solution)/shard_map/ppermute | solution.py:25
  658.2 22.4 %collective-permute-start.117 = (f32[1,16,128]{2,1,0:T(8,128)S(1)}, f32[1,16,128]{2,1,0:T(8,128)S(1)}, u32[]{:S(2)}, u32[]{:S(2)}) collective-permute-start(f32[1,16,128]{2,1,0:T(8,128)S(1)} %slice.1823), channel_id=1, source_target_pairs={{0,64},{1,65},{2,66},{3,67},{4,68},{5,69},{6,70},{7,71},{8,72},{9,... | collective-permute-start | bytes 24584 | tf_op jit(solution)/shard_map/ppermute | solution.py:25
  659.8 20.8 %collective-permute-start.116 = (f32[1,16,128]{2,1,0:T(8,128)S(1)}, f32[1,16,128]{2,1,0:T(8,128)S(1)}, u32[]{:S(2)}, u32[]{:S(2)}) collective-permute-start(f32[1,16,128]{2,1,0:T(8,128)S(1)} %slice.1822), channel_id=1, source_target_pairs={{64,0},{65,1},{66,2},{67,3},{68,4},{69,5},{70,6},{71,7},{72,8},{73... | collective-permute-start | bytes 24584 | tf_op jit(solution)/shard_map/ppermute | solution.py:25
  661.1 19.5 %collective-permute-start.118 = (f32[32,1,128]{2,1,0:T(1,128)S(1)}, f32[32,1,128]{2,1,0:T(1,128)S(1)}, u32[]{:S(2)}, u32[]{:S(2)}) collective-permute-start(f32[32,1,128]{2,1,0:T(1,128)S(1)} %slice.1828), channel_id=1, source_target_pairs={{2,0},{4,2},{6,4},{8,6},{10,8},{12,10},{14,12},{16,14},{18,16},{20... | collective-permute-start | bytes 49160 | tf_op jit(solution)/shard_map/ppermute | solution.py:25
  681.8 30.6 %collective-permute-start.130 = (f32[32,1,128]{2,1,0:T(1,128)S(1)}, f32[32,1,128]{2,1,0:T(1,128)S(1)}, u32[]{:S(2)}, u32[]{:S(2)}) collective-permute-start(f32[32,1,128]{2,1,0:T(1,128)S(1)} %slice.1862), channel_id=1, source_target_pairs={{2,0},{4,2},{6,4},{8,6},{10,8},{12,10},{14,12},{16,14},{18,16},{20... | collective-permute-start | bytes 49160 | tf_op jit(solution)/shard_map/ppermute | solution.py:25
  690.0 22.5 %collective-permute-start.131 = (f32[32,1,128]{2,1,0:T(1,128)S(1)}, f32[32,1,128]{2,1,0:T(1,128)S(1)}, u32[]{:S(2)}, u32[]{:S(2)}) collective-permute-start(f32[32,1,128]{2,1,0:T(1,128)S(1)} %slice.1863), channel_id=1, source_target_pairs={{0,2},{2,4},{4,6},{6,8},{8,10},{10,12},{12,14},{14,16},{16,18},{18... | collective-permute-start | bytes 49160 | tf_op jit(solution)/shard_map/ppermute | solution.py:25
  692.2 20.2 %collective-permute-start.128 = (f32[1,16,128]{2,1,0:T(8,128)S(1)}, f32[1,16,128]{2,1,0:T(8,128)S(1)}, u32[]{:S(2)}, u32[]{:S(2)}) collective-permute-start(f32[1,16,128]{2,1,0:T(8,128)S(1)} %slice.1856), channel_id=1, source_target_pairs={{64,0},{65,1},{66,2},{67,3},{68,4},{69,5},{70,6},{71,7},{72,8},{73... | collective-permute-start | bytes 24584 | tf_op jit(solution)/shard_map/ppermute | solution.py:25
  693.5 18.9 %collective-permute-start.129 = (f32[1,16,128]{2,1,0:T(8,128)S(1)}, f32[1,16,128]{2,1,0:T(8,128)S(1)}, u32[]{:S(2)}, u32[]{:S(2)}) collective-permute-start(f32[1,16,128]{2,1,0:T(8,128)S(1)} %slice.1857), channel_id=1, source_target_pairs={{0,64},{1,65},{2,66},{3,67},{4,68},{5,69},{6,70},{7,71},{8,72},{9,... | collective-permute-start | bytes 24584 | tf_op jit(solution)/shard_map/ppermute | solution.py:25
  (199 other events, 1819.4 us)
where the time goes:
time: 730 us; the launch traced here: 716 us
  starting transfers between devices  422 us (58%)
  other arithmetic  92.3 us (13%)
  waiting for transfers between devices  71 us (10%)
  blocking collectives  68.5 us (9%)
  local copies, waits for them, and re-layouts  52.9 us (7%)
  between operations  9.51 us (1%)
    ppermute x72, starting transfers between devices, passed_along(): return lax.ppermute(x, axis, pairs)  202 us
    ppermute x31, starting transfers between devices, with_halo(): after = lax.ppermute(first, axis, down)  115 us
    ppermute x31, starting transfers between devices, with_halo(): before = lax.ppermute(last, axis, up)  105 us
    psum x1, blocking collectives, local(): lax.psum((jnp.sum(pred_skel * label), jnp.sum(pred_skel), jnp.sum(label_s...  68.5 us
    ppermute x72, waiting for transfers between devices, passed_along(): return lax.ppermute(x, axis, pairs)  49.8 us
    gt x16, other arithmetic, pick(): take_low = lower > centre  20.3 us
    ppermute x31, waiting for transfers between devices, with_halo(): after = lax.ppermute(first, axis, down)  18.5 us
    select_n x12, other arithmetic, pick(): best = jnp.where(take_low, lower, centre)  15.3 us
  transfers between devices with their start and end apart: 134, of which 23 were waited for; matrix products, arithmetic and copies ran while one was open for 12% of the time, Pallas kernels for 0%

commit v1 on v0

v1 whole, which is shorter than its diff:
```python
import functools

import jax
import jax.numpy as jnp
from jax import lax
from jax.experimental import pallas as pl
from jax.experimental.pallas import tpu as pltpu
from jax.sharding import PartitionSpec as P

LEVELS = 6
Z, X, Y = 32, 16, 128
WIN = Z + 8
PAD = WIN + 16
ROWS = X + 16
GROUP = 16
LO = 4
SEMS = 64
MESH = pl.DeviceIdType.MESH

W, WL, WU = pl.ds(8, WIN), pl.ds(7, WIN), pl.ds(9, WIN)


def lane_of(v):
    return lax.broadcasted_iota(jnp.int32, v.shape, 1)


def plane_of(v):
    return lax.broadcasted_iota(jnp.int32, v.shape, 0)


def roll(v, by):
    return pltpu.roll(v, by, 1)


def max3(a, b, c):
    return jnp.maximum(jnp.maximum(a, b), c)


def route(g, best, candidates):
    zero = jnp.zeros_like(g)
    parts = []
    for value in candidates:
        hit = value == best
        parts.append(jnp.where(hit, g, zero))
        g = jnp.where(hit, zero, g)
    parts.append(g)
    return parts


def run(start, blocks, size, row):
    def block(b, _):
        todo, memo = [], {}
        first = start + b * size
        for q in range(size):
            todo += row(first + q, q, memo)
        for ref, at, value in todo:
            ref[at] = value
        return 0
    if isinstance(blocks, int) and blocks == 1:
        block(0, 0)
    else:
        lax.fori_loop(0, blocks, block, 0)


def once(memo, key, load):
    if key not in memo:
        memo[key] = load()
    return memo[key]


def kernel(nx, pred_hbm, label_hbm, out, loss, pred, label, in_sem, E, S, M1, M2, SM1, SM2, D, SP, SD, SSP, GB, SGB, SK, SSK,
           HX, SHX, HZ, G, SG, T, T2, SX, SX2, F, FO, RZ, RX, PS, PR, ARS, AR1, AR2S, AR2,
           send_sem, recv_sem, ar_send, ar_recv):
    gz, gx, gy = lax.axis_index("gz"), lax.axis_index("gx"), lax.axis_index("gy")
    prev, nxt = lax.rem(gx + nx - 1, nx), lax.rem(gx + 1, nx)
    nhi = nx // LO
    hi, lo = gx // LO, lax.rem(gx, LO)
    me1 = (gz * LO + lo) * 2 + gy
    o = pl.multiple_of(8 + 8 * gz, 8)
    O, OL, OU = pl.ds(o, Z), pl.ds(o - 1, Z), pl.ds(o + 1, Z)
    seam = 127 * (1 - gy)
    zlow = jnp.where(gz == 0, 0, -1)
    zhigh = jnp.where(gz == 1, Z - 1, -1)
    first_lane = jnp.where(gx == 0, 32, 0)
    last_lane = jnp.where(gx == nx - 1, 96, 128)

    def member(i):
        return (i // (2 * LO), hi * LO + lax.rem(i // 2, LO), lax.rem(i, 2))

    barrier = pltpu.get_barrier_semaphore()
    greet = [(gz, prev, gy), (gz, nxt, gy), (gz, prev, 1 - gy), (gz, nxt, 1 - gy)]
    greet += [member(lax.rem(me1 + d, GROUP)) for d in range(1, GROUP)]
    greet += [(gz, lax.rem(hi + d, nhi) * LO + lo, gy) for d in range(1, nhi)]
    for device in greet:
        pl.semaphore_signal(barrier, inc=1, device_id=device, device_id_type=MESH)

    loads = [pltpu.make_async_copy(src, dst, in_sem.at[f])
             for f, (src, dst) in enumerate(((pred_hbm, pred), (label_hbm, label)))]
    for load in loads:
        load.start()

    for f, ref in ((0, pred), (1, label)):
        loads[f].wait()

        def bring(x, _, memo, f=f, ref=ref):
            return [(E, (f, 0, 9 + x, pl.ds(o + 8 * t, 8)), ref[pl.ds(x + X * 8 * t, 8, stride=X), :])
                    for t in range(Z // 8)]
        run(0, 2, 8, bring)

    pl.semaphore_wait(barrier, len(greet))

    copies = []

    def send(number, src, dst, device):
        copy = pltpu.make_async_remote_copy(
            src_ref=src, dst_ref=dst, send_sem=send_sem.at[number], recv_sem=recv_sem.at[number],
            device_id=device, device_id_type=MESH)
        copy.start()
        copies.append(copy)
        return copy

    near = pl.multiple_of(32 - 16 * gz, 8)
    far = pl.multiple_of(8 + 32 * gz, 8)
    below, above = (gz, prev, gy), (gz, nxt, gy)
    arrived = [[], []]

    def pass_rows(f, base, planes):
        arrived[f] += [
            send(base, E.at[f, 0, pl.ds(9, 7), planes], E.at[f, 0, pl.ds(25, 7), planes], below),
            send(base + 1, E.at[f, 0, pl.ds(18, 7), planes], E.at[f, 0, pl.ds(2, 7), planes], above)]

    def first_halos(f):
        copy = send(8 * f, E.at[f, 0, pl.ds(9, X), pl.ds(near, 8)], E.at[f, 0, pl.ds(9, X), pl.ds(far, 8)],
                    (1 - gz, gx, gy))
        pass_rows(f, 8 * f + 1, O)
        return copy

    def second_halos(f, depth):
        depth.wait_recv()
        pass_rows(f, 8 * f + 3, pl.ds(pl.multiple_of(40 - 32 * gz, 8), 8))
        for half in (0, 1):
            packed = zero_w
            for i in range(8):
                v = E[f, 0, 9 + 8 * half + i, W]
                packed = jnp.where(lane_of(v) // 16 == i, roll(v, lax.rem(16 * i + 16 * (1 - gy), 128)), packed)
            PS[f, half] = packed
        arrived[f] += [
            send(8 * f + 5, PS.at[f], PR.at[f, pl.ds(1, 2)], (gz, gx, 1 - gy)),
            send(8 * f + 6, PS.at[f, 0], PR.at[f, 3], (gz, prev, 1 - gy)),
            send(8 * f + 7, PS.at[f, 1], PR.at[f, 0], (gz, nxt, 1 - gy))]

    zero_w = jnp.zeros((WIN, Y), jnp.float32)
    zero_o = jnp.zeros((Z, Y), jnp.float32)
    depth = first_halos(0)
    second_halos(0, depth)
    depth = first_halos(1)
    second_halos(1, depth)

    two = jnp.full((8, Y), 2.0, jnp.float32)

    def rims(r, _, memo):
        return [(E, (f, k, r, pl.ds(at, 8)), two)
                for f in (0, 1) for k in range(LEVELS + 1) for at in (0, PAD - 8)]
    run(0, 17, 2, rims)

    def strip_rims(j, _, memo):
        return [(S, (f, k, j, pl.ds(at, 8)), two)
                for f in (0, 1) for k in range(LEVELS + 1) for at in (0, PAD - 8)]
    run(1, 4, 2, strip_rims)
    run(0, 17, 2, lambda r, _, m: [(G, (p, q, r), zero_w) for p in (0, 1) for q in range(3)])
    run(0, 4, 8, lambda r, _, m: [(HZ, (r,), zero_w)])
    run(0, 2, 5, lambda j, _, m: [(SG, (p, q, j), zero_w) for p in (0, 1) for q in range(3)])
    run(0, 4, 5, lambda i, _, m: [(HX, (q, i), zero_o) for q in range(3)])
    run(0, 4, 4, lambda i, _, m: [(SK, (0, i), zero_o), (SK, (1, i), zero_o), (GB, (LEVELS, i + 1), zero_o)])
    run(0, 1, 8, lambda j, _, m: [(SSK, (j,), zero_o), (SGB, (LEVELS, j), zero_o)])
    for k in range(LEVELS + 1):
        GB[k, 0] = zero_o
        GB[k, X + 1] = zero_o
    for q in range(10):
        for p in range(3):
            T[q, p] = jnp.zeros((PAD, Y), jnp.float32)
        for p in range(2):
            T2[q, p] = jnp.zeros((PAD, Y), jnp.float32)
    for f in (0, 1):
        for r in (0, 1, ROWS, ROWS + 1):
            for k in range(LEVELS + 1) if r in (0, ROWS + 1) else (0,):
                E[f, k, r, W] = zero_w + 2.0

    def turn(r):
        return lax.rem(128 + 111 + 2 * gy - 32 * (r // 8), 128)

    def sides(v, seen):
        lane = lane_of(v)
        t = jnp.where(lane == seam, seen, v)
        return jnp.where(lane == 0, t, roll(v, 1)), jnp.where(lane == 127, t, roll(v, 127))

    def strip_sides(v):
        return roll(v, 1), roll(v, 127)

    def gather_sides(lower, upper, seen):
        lane = lane_of(lower)
        t = jnp.where(lane == seam, seen, 0.0)
        return jnp.where(lane == 127, t, roll(lower, 127)) + jnp.where(lane == 0, t, roll(upper, 1))

    def wrap_strip(ref, at, window, value):
        v = ref[at + (8, window)]
        v = jnp.where(lane_of(v) < first_lane, value, v)
        ref[at + (8, window)] = v
        ref[at + (0, window)] = roll(v, 32)
        v = ref[at + (1, window)]
        v = jnp.where(lane_of(v) >= last_lane, value, v)
        ref[at + (1, window)] = v
        ref[at + (9, window)] = roll(v, 96)

    def cap_rows(f, k):
        @pl.when(gx == 0)
        def _():
            E[f, k, 8, W] = zero_w + 2.0

        @pl.when(gx == nx - 1)
        def _():
            E[f, k, 25, W] = zero_w + 2.0

    def build_strip(f):
        def row(j, _, memo):
            acc = zero_w
            lane = lane_of(acc) // 16
            for g in range(4):
                own = roll(E[f, 0, 8 * g + j + 1, W], lax.rem(32 * g + 16, 128))
                other = roll(PR[f, g], lax.rem(32 * g - 16 * j + 16 * (1 - gy) + 128, 128))
                acc = jnp.where(lane == 2 * g + gy, own, acc)
                acc = jnp.where(lane == 2 * g + 1 - gy, other, acc)
            return [(S, (f, 0, j + 1, W), acc)]
        run(0, 2, 4, row)
        wrap_strip(S, (f, 0), W, 2.0)

    def eroded(ref, at, i, q, memo, pair):
        def centre(step):
            return once(memo, q + step, lambda: ref[at + (i + step, W)])
        c = centre(0)
        lower, upper = pair(c)
        m = jnp.minimum(jnp.minimum(c, lower), upper)
        m = jnp.minimum(m, jnp.minimum(ref[at + (i, WL)], ref[at + (i, WU)]))
        return jnp.minimum(m, jnp.minimum(centre(-1), centre(1)))

    def depth_max(ref, at, i):
        c = ref[at + (i, O)]
        plane = plane_of(c)
        lower = jnp.where(plane == zlow, c, ref[at + (i, OL)])
        upper = jnp.where(plane == zhigh, c, ref[at + (i, OU)])
        return max3(lower, c, upper)

    def level_forward(f, k, slot):
        start = jnp.where(k < 4, 1, 6)
        blocks = jnp.where(k < 4, 3, 2)

        def strip_erode(j, q, memo):
            return [(S, (f, k + 1, j + 1, W), eroded(S, (f, k), j + 1, q, memo, strip_sides))]
        run(0, 1, 8, strip_erode)
        wrap_strip(S, (f, k + 1), W, 2.0)

        def erode(r, q, memo):
            seen = roll(S[f, k, lax.rem(r, 8) + 1, W], turn(r))
            return [(E, (f, k + 1, r + 1, W), eroded(E, (f, k), r + 1, q, memo, lambda c: sides(c, seen)))]
        run(start, blocks, 10, erode)
        cap_rows(f, k + 1)

        def strip_depth(j, _, memo):
            return [(SM1, (slot, j + 1), depth_max(S, (f, k + 1), j + 1))]
        run(0, 1, 8, strip_depth)
        wrap_strip(SM1, (slot,), slice(None), 0.0)

        def strip_rows(j, q, memo):
            v = max3(*[once(memo, q + d, lambda d=d: SM1[slot, j + d]) for d in range(3)])
            todo = [(SM2, (slot, j), v)]
            if f == 0:
                lower, upper = strip_sides(v)
                delta = jnp.maximum(S[f, k, j + 1, O] - max3(lower, v, upper), 0.0)
                prior = SSK[j]
                todo += [(SD, (k, j), delta), (SSP, (k, j), prior),
                         (SSK, (j,), prior + jnp.maximum(delta - prior * delta, 0.0))]
            return todo
        run(0, 1, 8, strip_rows)

        def depth_rows(i, _, memo):
            return [(M1, (slot, i), depth_max(E, (f, k + 1), i + 8))]
        run(0, 2, 9, depth_rows)

        @pl.when(gx == 0)
        def _():
            M1[slot, 0] = zero_o

        @pl.when(gx == nx - 1)
        def _():
            M1[slot, X + 1] = zero_o

        def rest(i, q, memo):
            v = max3(*[once(memo, q + d, lambda d=d: M1[slot, i + d]) for d in range(3)])
            r = i + 8
            lower, upper = sides(v, roll(SM2[slot, lax.rem(r, 8)], turn(r)))
            delta = jnp.maximum(E[f, k, r + 1, O] - max3(lower, v, upper), 0.0)
            prior = SK[f, i]
            todo = [(M2, (slot, i), v), (SK, (f, i), prior + jnp.maximum(delta - prior * delta, 0.0))]
            if f == 0:
                todo += [(D, (k, i), delta), (SP, (k, i), prior)]
            return todo
        run(0, 2, 8, rest)

    def ar_copy(n, phase, slot, src, dst, number, device):
        return pltpu.make_async_remote_copy(
            src_ref=src, dst_ref=dst, send_sem=ar_send.at[n, phase, number], recv_sem=ar_recv.at[n, phase, slot],
            device_id=device, device_id_type=MESH)

    def ar_first(n, d):
        return ar_copy(n, 0, me1, ARS.at[n], AR1.at[n, me1], d, member(lax.rem(me1 + d, GROUP)))

    def ar_second(n, d):
        return ar_copy(n, 1, hi, AR2S.at[n], AR2.at[n, hi], d, (gz, lax.rem(hi + d, nhi) * LO + lo, gy))

    def ar_start(n, f):
        def add(b, carry):
            both, alone = carry
            for q in range(4):
                v = SK[f, 4 * b + q]
                both, alone = both + v * E[1 - f, 0, 4 * b + q + 9, O], alone + v
            return both, alone
        both, alone = lax.fori_loop(0, X // 4, add, (zero_o, zero_o))
        both = jnp.sum(both, axis=0, keepdims=True)
        alone = jnp.sum(alone, axis=0, keepdims=True)
        sub = plane_of(two)
        tile = jnp.where(sub == 0, both, jnp.where(sub == 1, alone, 0.0))
        ARS[n] = tile
        AR1[n, me1] = tile
        for d in range(1, GROUP):
            ar_first(n, d).start()

    def ar_middle(n):
        for d in range(1, GROUP):
            s = lax.rem(me1 + d, GROUP)
            ar_copy(n, 0, s, ARS.at[n], AR1.at[n, s], d, member(s)).wait_recv()
        tile = AR1[n, 0]
        for s in range(1, GROUP):
            tile = tile + AR1[n, s]
        AR2S[n] = tile
        AR2[n, hi] = tile
        for d in range(1, nhi):
            ar_second(n, d).start()

    def ar_end(n):
        for d in range(1, nhi):
            s = lax.rem(hi + d, nhi)
            ar_copy(n, 1, s, AR2S.at[n], AR2.at[n, s], d, (gz, s * LO + lo, gy)).wait_recv()
        tile = AR2[n, 0]
        for s in range(1, nhi):
            tile = tile + AR2[n, s]
        for d in range(1, GROUP):
            ar_first(n, d).wait_send()
        for d in range(1, nhi):
            ar_second(n, d).wait_send()
        tile = jnp.sum(tile, axis=1, keepdims=True)
        return tile[0:1], tile[1:2]

    for f in (0, 1):
        for copy in arrived[f]:
            copy.wait_recv()
        cap_rows(f, 0)
        build_strip(f)

        def level(k, _, f=f):
            level_forward(f, k, k if f == 0 else LEVELS)
            if f == 1:
                @pl.when(k == 2)
                def _():
                    ar_middle(0)
            return 0
        lax.fori_loop(0, LEVELS, level, 0)
        ar_start(f, f)

    both, alone = ar_end(0)
    pred_total = alone
    tprec = (both + 1.0) / (pred_total + 1.0)

    def chain(i, _, memo):
        t = E[1, 0, i + 9, O] - tprec
        todo = []
        for k in range(LEVELS - 1, -1, -1):
            delta, prior = D[k, i], SP[k, i]
            on = delta - prior * delta > 0
            GB[k, i + 1] = jnp.where(on, t * (1.0 - prior), 0.0)
            t = jnp.where(on, t * (1.0 - delta), t)
        return todo
    run(0, 4, 4, chain)

    def strip_chain(j, _, memo):
        t = S[1, 0, j + 1, O] - tprec
        lane = lane_of(t)
        mine = (lane >= 32) & (lane < 96)
        for k in range(LEVELS - 1, -1, -1):
            delta, prior = SD[k, j], SSP[k, j]
            on = delta - prior * delta > 0
            SGB[k, j] = jnp.where(on & mine, t * (1.0 - prior), 0.0)
            t = jnp.where(on, t * (1.0 - delta), t)
        return []
    run(0, 2, 4, strip_chain)

    def level_back(step, _):
        k = LEVELS - 1 - step
        old = lax.rem(step, 2)
        new = 1 - old

        start = jnp.where(k < 4, 1, 6)
        blocks = jnp.where(k < 4, 3, 2)

        def strip_cols(j, _, memo):
            a = SM2[k, j]
            lower, upper = strip_sides(a)
            gc, gl, gu = route(-SGB[k, j], max3(lower, a, upper), (a, lower))
            todo = [(SX, (0, j), gl), (SX, (1, j), gu)]
            g = gc + roll(gl, 127) + roll(gu, 1)
            gc, gl, gu = route(g, a, (SM1[k, j + 1], SM1[k, j]))
            return todo + [(SHX, (0, j + 1), gc), (SHX, (1, j + 1), gl), (SHX, (2, j + 1), gu)]
        run(0, 1, 8, strip_cols)
        SHX[1, 9] = roll(SHX[1, 1], 96)
        SHX[2, 0] = roll(SHX[2, 8], 32)

        def strip_depth(j, q, memo):
            g = SHX[0, j + 1] + SHX[1, j + 2] + SHX[2, j]
            gc, gl, gu = route(g, SM1[k, j + 1], (S[0, k + 1, j + 1, O], S[0, k + 1, j + 1, OL]))
            T[q, 0, O] = gc + SGB[k + 1, j]
            T[q, 1, O] = gl
            T[q, 2, O] = gu
            g = SG[old, 0, j + 1] + SG[old, 1, j + 2] + SG[old, 2, j]
            g = g + T[q, 0, W] + T[q, 1, WU] + T[q, 2, WL]
            c = S[0, k, j + 1, W]
            lower, upper = strip_sides(c)
            gc, zl, zu, xl, xu, yl, yu = route(
                g, S[0, k + 1, j + 1, W],
                (c, S[0, k, j + 1, WL], S[0, k, j + 1, WU], S[0, k, j, W], S[0, k, j + 2, W], lower))
            T2[q, 0, W] = zl
            T2[q, 1, W] = zu
            return [(SX2, (0, j), yl), (SX2, (1, j), yu),
                    (SG, (new, 0, j + 1), gc + roll(yl, 127) + roll(yu, 1) + T2[q, 0, WU] + T2[q, 1, WL]),
                    (SG, (new, 1, j + 1), xl), (SG, (new, 2, j + 1), xu)]
        run(0, 1, 8, strip_depth)
        SG[new, 1, 9] = roll(SG[new, 1, 1], 96)
        SG[new, 2, 0] = roll(SG[new, 2, 8], 32)

        def cols(i, _, memo):
            a = M2[k, i]
            r = i + 8
            by, j = turn(r), lax.rem(r, 8)
            lower, upper = sides(a, roll(SM2[k, j], by))
            gc, gl, gu = route(-GB[k, i + 1], max3(lower, a, upper), (a, lower))
            g = gc + gather_sides(gl, gu, roll(SX[gy, j], by))
            gc, gl, gu = route(g, a, (M1[k, i + 1], M1[k, i]))
            return [(HX, (0, i + 2), gc), (HX, (1, i + 2), gl), (HX, (2, i + 2), gu)]
        run(0, 2, 8, cols)

        def depths(i, q, memo):
            g = HX[0, i + 1] + HX[1, i + 2] + HX[2, i]
            gc, gl, gu = route(g, M1[k, i], (E[0, k + 1, i + 8, O], E[0, k + 1, i + 8, OL]))
            T[q, 0, O] = gc + GB[k + 1, i]
            T[q, 1, O] = gl
            T[q, 2, O] = gu
            return [(HZ, (i + 7,), T[q, 0, W] + T[q, 1, WU] + T[q, 2, WL])]
        run(0, 2, 9, depths)

        def back(r, q, memo):
            g = G[old, 0, r + 1] + G[old, 1, r + 2] + G[old, 2, r] + HZ[r]
            by, j = turn(r), lax.rem(r, 8)
            below, c, above = [once(memo, q + d, lambda d=d: E[0, k, r + d, W]) for d in range(3)]
            lower, upper = sides(c, roll(S[0, k, j + 1, W], by))
            gc, zl, zu, xl, xu, yl, yu = route(
                g, E[0, k + 1, r + 1, W],
                (c, E[0, k, r + 1, WL], E[0, k, r + 1, WU], below, above, lower))
            T2[q, 0, W] = zl
            T2[q, 1, W] = zu
            return [(G, (new, 0, r + 1), gc + gather_sides(yl, yu, roll(SX2[gy, j], by)) + T2[q, 0, WU] + T2[q, 1, WL]),
                    (G, (new, 1, r + 1), xl), (G, (new, 2, r + 1), xu)]
        run(start, blocks, 10, back)

        @pl.when(step == 2)
        def _():
            ar_middle(1)
        return 0
    lax.fori_loop(0, LEVELS, level_back, 0)

    last = LEVELS % 2

    def total(r, _, memo):
        return [(F, (r,), G[last, 0, r + 1] + G[last, 1, r + 2] + G[last, 2, r])]
    run(0, 4, 8, total)
    beyond = pl.multiple_of(32 - 32 * gz, 8)
    mine = pl.multiple_of(8 * gz, 8)
    inner = pl.multiple_of(24 - 24 * gz, 8)
    rest_at = pl.multiple_of(8 * gz, 8)
    quiet = pl.ds(rest_at, Z - 8)
    edge = pl.ds(inner, 8)
    copy = send(16, F.at[pl.ds(1, 30), pl.ds(beyond, 8)], RZ.at[pl.ds(1, 30)], (1 - gz, gx, gy))
    back_rows = []

    def return_rows(base, planes):
        back_rows.append(send(base, FO.at[pl.ds(1, 7), planes], RX.at[0, :, planes], below))
        back_rows.append(send(base + 1, FO.at[pl.ds(24, 7), planes], RX.at[1, :, planes], above))

    run(1, 5, 6, lambda r, _, m: [(FO, (r,), F[r, pl.ds(mine, Z)])])
    return_rows(17, quiet)
    copy.wait_recv()
    run(1, 5, 6, lambda r, _, m: [(FO, (r, edge), F[r, pl.ds(mine + inner, 8)] + RZ[r])])
    return_rows(19, edge)

    both, alone = ar_end(1)
    tsens = (both + 1.0) / (alone + 1.0)
    square = (tprec + tsens) * (tprec + tsens)
    voxels = float(2 * nx * 2 * Z * X * Y)
    by_prec = -2.0 * tsens * tsens / square / (pred_total + 1.0) * voxels
    by_sens = -2.0 * tprec * tprec / square / (alone + 1.0) * voxels
    loss[...] = 1.0 - 2.0 * tprec * tsens / (tprec + tsens)

    for copy in back_rows:
        copy.wait_recv()

    def give(x, _, memo, extra):
        g = FO[x + 8] + GB[0, x + 1]
        if extra is not None:
            g = g + extra(x)
        g = g * by_prec + SK[1, x] * by_sens
        return [(out, (pl.ds(x + X * 8 * t, 8, stride=X), slice(None)), g[8 * t:8 * t + 8]) for t in range(Z // 8)]
    run(0, 1, 7, functools.partial(give, extra=lambda x: RX[1, x]))
    run(7, 1, 2, functools.partial(give, extra=None))
    run(9, 1, 7, functools.partial(give, extra=lambda x: RX[0, x - 9]))
    for copy in copies:
        copy.wait_send()


def local(prediction, label):
    nx = lax.axis_size("gx")
    nhi = nx // LO
    f32 = jnp.float32

    def vmem(*shape):
        return pltpu.VMEM(shape + (Y,), f32)

    grad, loss = pl.pallas_call(
        functools.partial(kernel, nx),
        out_shape=(jax.ShapeDtypeStruct((Z * X, Y), f32), jax.ShapeDtypeStruct((1, 1), f32)),
        in_specs=[pl.BlockSpec(memory_space=pl.ANY)] * 2,
        out_specs=[pl.BlockSpec(memory_space=pltpu.VMEM)] * 2,
        scratch_shapes=[
            vmem(Z * X), vmem(Z * X), pltpu.SemaphoreType.DMA((2,)),
            vmem(2, 7, ROWS + 2, PAD), vmem(2, 7, 10, PAD),
            vmem(7, X + 2, Z), vmem(7, X, Z), vmem(7, 10, Z), vmem(7, 8, Z),
            vmem(6, X, Z), vmem(6, X, Z), vmem(6, 8, Z), vmem(6, 8, Z),
            vmem(7, X + 2, Z), vmem(7, 8, Z),
            vmem(2, X, Z), vmem(8, Z),
            vmem(3, X + 4, Z), vmem(3, 10, Z), vmem(ROWS, WIN),
            vmem(2, 3, ROWS + 2, WIN), vmem(2, 3, 10, WIN),
            vmem(10, 3, PAD), vmem(10, 2, PAD), vmem(2, 8, Z), vmem(2, 8, WIN),
            vmem(ROWS, WIN), vmem(ROWS, Z), vmem(ROWS, 8), vmem(2, 7, Z),
            vmem(2, 2, WIN), vmem(2, 4, WIN),
            vmem(2, 8), vmem(2, GROUP, 8), vmem(2, 8), vmem(2, nhi, 8),
            pltpu.SemaphoreType.DMA((21,)), pltpu.SemaphoreType.DMA((21,)),
            pltpu.SemaphoreType.DMA((2, 2, GROUP)), pltpu.SemaphoreType.DMA((2, 2, GROUP)),
        ],
        compiler_params=pltpu.CompilerParams(
            collective_id=0, has_side_effects=True, vmem_limit_bytes=56 * 1024 * 1024),
    )(prediction.reshape(Z * X, Y), label.reshape(Z * X, Y))
    return loss.reshape(()), grad.reshape(Z, X, Y)


def solution(mesh):
    in_specs = (P("gz", "gx", "gy"), P("gz", "gx", "gy"))
    out_specs = (P(), P("gz", "gx", "gy"))
    return jax.shard_map(local, mesh=mesh, in_specs=in_specs, out_specs=out_specs, check_vma=False)
```

time: 730 us -> 79.5 us (0.11)
  the two profiles are of different devices: /device:TPU:32 before, /device:TPU:0 now
where the time goes in v1:
time: 79.5 us; the launch traced here: 79.4 us
  Pallas kernels  75.3 us (95%)
  between operations  2.4 us (3%)
  local copies, waits for them, and re-layouts  1.67 us (2%)
    pallas_call x1, Pallas kernels, local(): pl.pallas_call(functools.partial(kernel, nx), out_shape=(jax.ShapeDtypeSt...  75.3 us
    unnamed x1, local copies, waits for them, and re-layouts  1.67 us

profile of v1, /device:TPU:0, one launch (start us, length us, event | category | flops | bytes accessed | tf_op | source)
XLA Modules:
  0.0 79.4 jit_solution(11860836623829351682)
XLA Ops:
  0.6 75.3 %shard_map.41 = (f32[512,128]{1,0:T(8,128)}, f32[1,1]{1,0:T(1,128)}) custom-call(f32[512,128]{1,0:T(8,128)} %bitcast.4, f32[512,128]{1,0:T(8,128)} %bitcast.5), custom_call_target="tpu_custom_call" | custom-call | tf_op jit(solution)/shard_map/pallas_call | solution.py:544
  76.6 1.7 %copy.7 = f32[32,16,128]{2,1,0:T(8,128)} copy(f32[32,16,128]{2,1,0:T(8,128)} %bitcast.6) | data formatting | bytes 524288

commit v2 on v1

--- a/solution.py
+++ b/solution.py
@@ -50,7 +50,7 @@
 def run(start, blocks, size, row):
     def block(b, _):
         todo, memo = [], {}
-        first = start + b * size
+        first = start(b) if callable(start) else start + b * size
         for q in range(size):
             todo += row(first + q, q, memo)
         for ref, at, value in todo:
@@ -66,6 +66,14 @@
     if key not in memo:
         memo[key] = load()
     return memo[key]
+
+
+def slot_of(f, k):
+    if f == 0:
+        return k
+    if isinstance(k, int) and k == 0:
+        return 7
+    return jnp.where(k == 0, 7, 8 + lax.rem(k, 2))
 
 
 def kernel(nx, pred_hbm, label_hbm, out, loss, pred, label, in_sem, E, S, M1, M2, SM1, SM2, D, SP, SD, SSP, GB, SGB, SK, SSK,
@@ -88,8 +96,13 @@
         return (i // (2 * LO), hi * LO + lax.rem(i // 2, LO), lax.rem(i, 2))
 
     barrier = pltpu.get_barrier_semaphore()
-    greet = [(gz, prev, gy), (gz, nxt, gy), (gz, prev, 1 - gy), (gz, nxt, 1 - gy)]
-    greet += [member(lax.rem(me1 + d, GROUP)) for d in range(1, GROUP)]
+    has_prev, has_nxt = gx > 0, gx < nx - 1
+    for inside, row in ((has_prev, prev), (has_nxt, nxt)):
+        @pl.when(inside)
+        def _(row=row):
+            for cols in (gy, 1 - gy):
+                pl.semaphore_signal(barrier, inc=1, device_id=(gz, row, cols), device_id_type=MESH)
+    greet = [member(lax.rem(me1 + d, GROUP)) for d in range(1, GROUP)]
     greet += [(gz, lax.rem(hi + d, nhi) * LO + lo, gy) for d in range(1, nhi)]
     for device in greet:
         pl.semaphore_signal(barrier, inc=1, device_id=device, device_id_type=MESH)
@@ -103,21 +116,45 @@
         loads[f].wait()
 
         def bring(x, _, memo, f=f, ref=ref):
-            return [(E, (f, 0, 9 + x, pl.ds(o + 8 * t, 8)), ref[pl.ds(x + X * 8 * t, 8, stride=X), :])
+            return [(E, (7 * f, 9 + x, pl.ds(o + 8 * t, 8)), ref[pl.ds(x + X * 8 * t, 8, stride=X), :])
                     for t in range(Z // 8)]
         run(0, 2, 8, bring)
 
-    pl.semaphore_wait(barrier, len(greet))
+    zero_w = jnp.zeros((WIN, Y), jnp.float32)
+    zero_o = jnp.zeros((Z, Y), jnp.float32)
+    pl.semaphore_wait(barrier, len(greet) + jnp.where(has_prev, 2, 0) + jnp.where(has_nxt, 2, 0))
 
     copies = []
 
-    def send(number, src, dst, device):
+    def only(inside, act):
+        if inside is None:
+            act()
+        else:
+            pl.when(inside)(act)
+
+    class Sent:
+        def __init__(self, copy, sends, gets):
+            self.copy, self.sends, self.gets = copy, sends, gets
+
+        def start(self):
+            only(self.sends, self.copy.start)
+
+        def wait_recv(self):
+            only(self.gets, self.copy.wait_recv)
+
+        def wait_send(self):
+            only(self.sends, self.copy.wait_send)
+
+    def send(number, src, dst, device, step=0, now=True):
         copy = pltpu.make_async_remote_copy(
             src_ref=src, dst_ref=dst, send_sem=send_sem.at[number], recv_sem=recv_sem.at[number],
             device_id=device, device_id_type=MESH)
-        copy.start()
-        copies.append(copy)
-        return copy
+        sends = {0: None, -1: has_prev, 1: has_nxt}[step]
+        gets = {0: None, -1: has_nxt, 1: has_prev}[step]
+        copies.append(Sent(copy, sends, gets))
+        if now:
+            copies[-1].start()
+        return copies[-1]
 
     near = pl.multiple_of(32 - 16 * gz, 8)
     far = pl.multiple_of(8 + 32 * gz, 8)
@@ -126,11 +163,11 @@
 
     def pass_rows(f, base, planes):
         arrived[f] += [
-            send(base, E.at[f, 0, pl.ds(9, 7), planes], E.at[f, 0, pl.ds(25, 7), planes], below),
-            send(base + 1, E.at[f, 0, pl.ds(18, 7), planes], E.at[f, 0, pl.ds(2, 7), planes], above)]
+            send(base, E.at[7 * f, pl.ds(9, 7), planes], E.at[7 * f, pl.ds(25, 7), planes], below, -1),
+            send(base + 1, E.at[7 * f, pl.ds(18, 7), planes], E.at[7 * f, pl.ds(2, 7), planes], above, 1)]
 
     def first_halos(f):
-        copy = send(8 * f, E.at[f, 0, pl.ds(9, X), pl.ds(near, 8)], E.at[f, 0, pl.ds(9, X), pl.ds(far, 8)],
+        copy = send(8 * f, E.at[7 * f, pl.ds(9, X), pl.ds(near, 8)], E.at[7 * f, pl.ds(9, X), pl.ds(far, 8)],
                     (1 - gz, gx, gy))
         pass_rows(f, 8 * f + 1, O)
         return copy
@@ -141,16 +178,14 @@
         for half in (0, 1):
             packed = zero_w
             for i in range(8):
-                v = E[f, 0, 9 + 8 * half + i, W]
+                v = E[7 * f, 9 + 8 * half + i, W]
                 packed = jnp.where(lane_of(v) // 16 == i, roll(v, lax.rem(16 * i + 16 * (1 - gy), 128)), packed)
             PS[f, half] = packed
         arrived[f] += [
             send(8 * f + 5, PS.at[f], PR.at[f, pl.ds(1, 2)], (gz, gx, 1 - gy)),
-            send(8 * f + 6, PS.at[f, 0], PR.at[f, 3], (gz, prev, 1 - gy)),
-            send(8 * f + 7, PS.at[f, 1], PR.at[f, 0], (gz, nxt, 1 - gy))]
-
-    zero_w = jnp.zeros((WIN, Y), jnp.float32)
-    zero_o = jnp.zeros((Z, Y), jnp.float32)
+            send(8 * f + 6, PS.at[f, 0], PR.at[f, 3], (gz, prev, 1 - gy), -1),
+            send(8 * f + 7, PS.at[f, 1], PR.at[f, 0], (gz, nxt, 1 - gy), 1)]
+
     depth = first_halos(0)
     second_halos(0, depth)
     depth = first_halos(1)
@@ -159,16 +194,15 @@
     two = jnp.full((8, Y), 2.0, jnp.float32)
 
     def rims(r, _, memo):
-        return [(E, (f, k, r, pl.ds(at, 8)), two)
-                for f in (0, 1) for k in range(LEVELS + 1) for at in (0, PAD - 8)]
+        return [(E, (slot, r, pl.ds(at, 8)), two) for slot in range(10) for at in (0, PAD - 8)]
     run(0, 17, 2, rims)
 
     def strip_rims(j, _, memo):
         return [(S, (f, k, j, pl.ds(at, 8)), two)
                 for f in (0, 1) for k in range(LEVELS + 1) for at in (0, PAD - 8)]
     run(1, 4, 2, strip_rims)
-    run(0, 17, 2, lambda r, _, m: [(G, (p, q, r), zero_w) for p in (0, 1) for q in range(3)])
-    run(0, 4, 8, lambda r, _, m: [(HZ, (r,), zero_w)])
+    run(0, 17, 2, lambda r, _, m: [(G, (p, q, r), zero_w) for p in range(LEVELS + 1) for q in range(3)])
+    run(0, 4, 8, lambda r, _, m: [(HZ, (k, r), zero_w) for k in range(LEVELS)])
     run(0, 2, 5, lambda j, _, m: [(SG, (p, q, j), zero_w) for p in (0, 1) for q in range(3)])
     run(0, 4, 5, lambda i, _, m: [(HX, (q, i), zero_o) for q in range(3)])
     run(0, 4, 4, lambda i, _, m: [(SK, (0, i), zero_o), (SK, (1, i), zero_o), (GB, (LEVELS, i + 1), zero_o)])
@@ -181,10 +215,25 @@
             T[q, p] = jnp.zeros((PAD, Y), jnp.float32)
         for p in range(2):
             T2[q, p] = jnp.zeros((PAD, Y), jnp.float32)
-    for f in (0, 1):
-        for r in (0, 1, ROWS, ROWS + 1):
-            for k in range(LEVELS + 1) if r in (0, ROWS + 1) else (0,):
-                E[f, k, r, W] = zero_w + 2.0
+    for r in (0, 1, ROWS, ROWS + 1):
+        for slot in range(10) if r in (0, ROWS + 1) else (0, 7):
+            E[slot, r, W] = zero_w + 2.0
+
+    @pl.when(gx == 0)
+    def _():
+        for f in (0, 1):
+            PR[f, 0] = zero_w + 2.0
+            for r in range(2, 9):
+                E[7 * f, r, W] = zero_w + 2.0
+        RX[1] = jnp.zeros((7, Z, Y), jnp.float32)
+
+    @pl.when(gx == nx - 1)
+    def _():
+        for f in (0, 1):
+            PR[f, 3] = zero_w + 2.0
+            for r in range(25, 32):
+                E[7 * f, r, W] = zero_w + 2.0
+        RX[0] = jnp.zeros((7, Z, Y), jnp.float32)
 
     def turn(r):
         return lax.rem(128 + 111 + 2 * gy - 32 * (r // 8), 128)
@@ -215,18 +264,18 @@
     def cap_rows(f, k):
         @pl.when(gx == 0)
         def _():
-            E[f, k, 8, W] = zero_w + 2.0
+            E[slot_of(f, k), 8, W] = zero_w + 2.0
 
         @pl.when(gx == nx - 1)
         def _():
-            E[f, k, 25, W] = zero_w + 2.0
+            E[slot_of(f, k), 25, W] = zero_w + 2.0
 
     def build_strip(f):
         def row(j, _, memo):
             acc = zero_w
             lane = lane_of(acc) // 16
             for g in range(4):
-                own = roll(E[f, 0, 8 * g + j + 1, W], lax.rem(32 * g + 16, 128))
+                own = roll(E[7 * f, 8 * g + j + 1, W], lax.rem(32 * g + 16, 128))
                 other = roll(PR[f, g], lax.rem(32 * g - 16 * j + 16 * (1 - gy) + 128, 128))
                 acc = jnp.where(lane == 2 * g + gy, own, acc)
                 acc = jnp.where(lane == 2 * g + 1 - gy, other, acc)
@@ -261,7 +310,7 @@
 
         def erode(r, q, memo):
             seen = roll(S[f, k, lax.rem(r, 8) + 1, W], turn(r))
-            return [(E, (f, k + 1, r + 1, W), eroded(E, (f, k), r + 1, q, memo, lambda c: sides(c, seen)))]
+            return [(E, (slot_of(f, k + 1), r + 1, W), eroded(E, (slot_of(f, k),), r + 1, q, memo, lambda c: sides(c, seen)))]
         run(start, blocks, 10, erode)
         cap_rows(f, k + 1)
 
@@ -283,7 +332,7 @@
         run(0, 1, 8, strip_rows)
 
         def depth_rows(i, _, memo):
-            return [(M1, (slot, i), depth_max(E, (f, k + 1), i + 8))]
+            return [(M1, (slot, i), depth_max(E, (slot_of(f, k + 1),), i + 8))]
         run(0, 2, 9, depth_rows)
 
         @pl.when(gx == 0)
@@ -298,7 +347,7 @@
             v = max3(*[once(memo, q + d, lambda d=d: M1[slot, i + d]) for d in range(3)])
             r = i + 8
             lower, upper = sides(v, roll(SM2[slot, lax.rem(r, 8)], turn(r)))
-            delta = jnp.maximum(E[f, k, r + 1, O] - max3(lower, v, upper), 0.0)
+            delta = jnp.maximum(E[slot_of(f, k), r + 1, O] - max3(lower, v, upper), 0.0)
             prior = SK[f, i]
             todo = [(M2, (slot, i), v), (SK, (f, i), prior + jnp.maximum(delta - prior * delta, 0.0))]
             if f == 0:
@@ -322,7 +371,7 @@
             both, alone = carry
             for q in range(4):
                 v = SK[f, 4 * b + q]
-                both, alone = both + v * E[1 - f, 0, 4 * b + q + 9, O], alone + v
+                both, alone = both + v * E[7 - 7 * f, 4 * b + q + 9, O], alone + v
             return both, alone
         both, alone = lax.fori_loop(0, X // 4, add, (zero_o, zero_o))
         both = jnp.sum(both, axis=0, keepdims=True)
@@ -381,7 +430,7 @@
     tprec = (both + 1.0) / (pred_total + 1.0)
 
     def chain(i, _, memo):
-        t = E[1, 0, i + 9, O] - tprec
+        t = E[7, i + 9, O] - tprec
         todo = []
         for k in range(LEVELS - 1, -1, -1):
             delta, prior = D[k, i], SP[k, i]
@@ -403,19 +452,16 @@
         return []
     run(0, 2, 4, strip_chain)
 
-    def level_back(step, _):
+    def strip_back(step, _):
         k = LEVELS - 1 - step
         old = lax.rem(step, 2)
         new = 1 - old
-
-        start = jnp.where(k < 4, 1, 6)
-        blocks = jnp.where(k < 4, 3, 2)
 
         def strip_cols(j, _, memo):
             a = SM2[k, j]
             lower, upper = strip_sides(a)
             gc, gl, gu = route(-SGB[k, j], max3(lower, a, upper), (a, lower))
-            todo = [(SX, (0, j), gl), (SX, (1, j), gu)]
+            todo = [(SX, (k, 0, j), gl), (SX, (k, 1, j), gu)]
             g = gc + roll(gl, 127) + roll(gu, 1)
             gc, gl, gu = route(g, a, (SM1[k, j + 1], SM1[k, j]))
             return todo + [(SHX, (0, j + 1), gc), (SHX, (1, j + 1), gl), (SHX, (2, j + 1), gu)]
@@ -438,76 +484,113 @@
                 (c, S[0, k, j + 1, WL], S[0, k, j + 1, WU], S[0, k, j, W], S[0, k, j + 2, W], lower))
             T2[q, 0, W] = zl
             T2[q, 1, W] = zu
-            return [(SX2, (0, j), yl), (SX2, (1, j), yu),
+            return [(SX2, (k, 0, j), yl), (SX2, (k, 1, j), yu),
                     (SG, (new, 0, j + 1), gc + roll(yl, 127) + roll(yu, 1) + T2[q, 0, WU] + T2[q, 1, WL]),
                     (SG, (new, 1, j + 1), xl), (SG, (new, 2, j + 1), xu)]
-        run(0, 1, 8, strip_depth)
+        run(0, 2, 4, strip_depth)
         SG[new, 1, 9] = roll(SG[new, 1, 1], 96)
         SG[new, 2, 0] = roll(SG[new, 2, 8], 32)
-
+        return 0
+    lax.fori_loop(0, LEVELS, strip_back, 0)
+
+    def open_back(k, _):
         def cols(i, _, memo):
             a = M2[k, i]
             r = i + 8
             by, j = turn(r), lax.rem(r, 8)
             lower, upper = sides(a, roll(SM2[k, j], by))
             gc, gl, gu = route(-GB[k, i + 1], max3(lower, a, upper), (a, lower))
-            g = gc + gather_sides(gl, gu, roll(SX[gy, j], by))
+            g = gc + gather_sides(gl, gu, roll(SX[k, gy, j], by))
             gc, gl, gu = route(g, a, (M1[k, i + 1], M1[k, i]))
             return [(HX, (0, i + 2), gc), (HX, (1, i + 2), gl), (HX, (2, i + 2), gu)]
         run(0, 2, 8, cols)
 
         def depths(i, q, memo):
             g = HX[0, i + 1] + HX[1, i + 2] + HX[2, i]
-            gc, gl, gu = route(g, M1[k, i], (E[0, k + 1, i + 8, O], E[0, k + 1, i + 8, OL]))
+            gc, gl, gu = route(g, M1[k, i], (E[k + 1, i + 8, O], E[k + 1, i + 8, OL]))
             T[q, 0, O] = gc + GB[k + 1, i]
             T[q, 1, O] = gl
             T[q, 2, O] = gu
-            return [(HZ, (i + 7,), T[q, 0, W] + T[q, 1, WU] + T[q, 2, WL])]
-        run(0, 2, 9, depths)
-
-        def back(r, q, memo):
-            g = G[old, 0, r + 1] + G[old, 1, r + 2] + G[old, 2, r] + HZ[r]
-            by, j = turn(r), lax.rem(r, 8)
-            below, c, above = [once(memo, q + d, lambda d=d: E[0, k, r + d, W]) for d in range(3)]
-            lower, upper = sides(c, roll(S[0, k, j + 1, W], by))
-            gc, zl, zu, xl, xu, yl, yu = route(
-                g, E[0, k + 1, r + 1, W],
-                (c, E[0, k, r + 1, WL], E[0, k, r + 1, WU], below, above, lower))
-            T2[q, 0, W] = zl
-            T2[q, 1, W] = zu
-            return [(G, (new, 0, r + 1), gc + gather_sides(yl, yu, roll(SX2[gy, j], by)) + T2[q, 0, WU] + T2[q, 1, WL]),
-                    (G, (new, 1, r + 1), xl), (G, (new, 2, r + 1), xu)]
-        run(start, blocks, 10, back)
-
-        @pl.when(step == 2)
+            return [(HZ, (k, i + 7), T[q, 0, W] + T[q, 1, WU] + T[q, 2, WL])]
+        run(0, 3, 6, depths)
+
+        @pl.when(k == 2)
         def _():
             ar_middle(1)
         return 0
-    lax.fori_loop(0, LEVELS, level_back, 0)
-
-    last = LEVELS % 2
-
-    def total(r, _, memo):
-        return [(F, (r,), G[last, 0, r + 1] + G[last, 1, r + 2] + G[last, 2, r])]
-    run(0, 4, 8, total)
+    lax.fori_loop(0, LEVELS, open_back, 0)
+
+    def erode_back(k, r, q, memo):
+        g = G[k + 1, 0, r + 1] + G[k + 1, 1, r + 2] + G[k + 1, 2, r] + HZ[k, r]
+        by, j = turn(r), lax.rem(r, 8)
+        under, c, over = [once(memo, q + d, lambda d=d: E[k, r + d, W]) for d in range(3)]
+        lower, upper = sides(c, roll(S[0, k, j + 1, W], by))
+        gc, zl, zu, xl, xu, yl, yu = route(
+            g, E[k + 1, r + 1, W],
+            (c, E[k, r + 1, WL], E[k, r + 1, WU], under, over, lower))
+        T2[q, 0, W] = zl
+        T2[q, 1, W] = zu
+        return [(G, (k, 0, r + 1), gc + gather_sides(yl, yu, roll(SX2[k, gy, j], by)) + T2[q, 0, WU] + T2[q, 1, WL]),
+                (G, (k, 1, r + 1), xl), (G, (k, 2, r + 1), xu)]
+
+    def outer(step, _):
+        k = LEVELS - 1 - step
+        run(lambda b: jnp.where(b < 2, 1 + k + 4 * b, 15 - k + 4 * b), 4, 4, lambda r, q, memo: erode_back(k, r, q, memo))
+        return 0
+    lax.fori_loop(0, LEVELS, outer, 0)
+
     beyond = pl.multiple_of(32 - 32 * gz, 8)
     mine = pl.multiple_of(8 * gz, 8)
     inner = pl.multiple_of(24 - 24 * gz, 8)
-    rest_at = pl.multiple_of(8 * gz, 8)
-    quiet = pl.ds(rest_at, Z - 8)
+    quiet = pl.ds(mine, Z - 8)
     edge = pl.ds(inner, 8)
-    copy = send(16, F.at[pl.ds(1, 30), pl.ds(beyond, 8)], RZ.at[pl.ds(1, 30)], (1 - gz, gx, gy))
     back_rows = []
 
-    def return_rows(base, planes):
-        back_rows.append(send(base, FO.at[pl.ds(1, 7), planes], RX.at[0, :, planes], below))
-        back_rows.append(send(base + 1, FO.at[pl.ds(24, 7), planes], RX.at[1, :, planes], above))
-
-    run(1, 5, 6, lambda r, _, m: [(FO, (r,), F[r, pl.ds(mine, Z)])])
-    return_rows(17, quiet)
+    def total(r, _, memo):
+        v = G[0, 0, r + 1] + G[0, 1, r + 2] + G[0, 2, r]
+        return [(F, (r,), v)]
+
+    def from_depth(r, _, memo):
+        return [(FO, (r, edge), F[r, pl.ds(mine + inner, 8)] + RZ[r])]
+
+    def own_planes(r, _, memo):
+        return [(FO, (r,), F[r, pl.ds(mine, Z)])]
+
+    def return_rows(base, planes, now):
+        back_rows.append(send(base, FO.at[pl.ds(1, 7), planes], RX.at[0, :, planes], below, -1, now))
+        back_rows.append(send(base + 1, FO.at[pl.ds(24, 7), planes], RX.at[1, :, planes], above, 1, now))
+
+    def to_depth(number, rows):
+        return send(number, F.at[rows, pl.ds(beyond, 8)], RZ.at[rows], (1 - gz, gx, gy))
+
+    for start in (1, 24):
+        run(start, 1, 7, total)
+    margin = [to_depth(16, pl.ds(1, 7)), to_depth(17, pl.ds(24, 7))]
+    for start in (1, 24):
+        run(start, 1, 7, own_planes)
+    return_rows(18, quiet, True)
+    return_rows(20, edge, False)
+
+    def inside(step, _):
+        k = LEVELS - 1 - step
+        at = (k + 1) // 2
+        run(8 + 2 * at, 4 - at, 4, lambda r, q, memo: erode_back(k, r, q, memo))
+
+        @pl.when(step == 1)
+        def _():
+            for copy in margin:
+                copy.wait_recv()
+            for start in (1, 24):
+                run(start, 1, 7, from_depth)
+            for copy in back_rows[2:]:
+                copy.start()
+        return 0
+    lax.fori_loop(0, LEVELS, inside, 0)
+    run(8, 2, 8, total)
+    copy = to_depth(22, pl.ds(8, 16))
+    run(8, 2, 8, own_planes)
     copy.wait_recv()
-    run(1, 5, 6, lambda r, _, m: [(FO, (r, edge), F[r, pl.ds(mine + inner, 8)] + RZ[r])])
-    return_rows(19, edge)
+    run(8, 2, 8, from_depth)
 
     both, alone = ar_end(1)
     tsens = (both + 1.0) / (alone + 1.0)
@@ -548,18 +631,18 @@
         out_specs=[pl.BlockSpec(memory_space=pltpu.VMEM)] * 2,
         scratch_shapes=[
             vmem(Z * X), vmem(Z * X), pltpu.SemaphoreType.DMA((2,)),
-            vmem(2, 7, ROWS + 2, PAD), vmem(2, 7, 10, PAD),
+            vmem(10, ROWS + 2, PAD), vmem(2, 7, 10, PAD),
             vmem(7, X + 2, Z), vmem(7, X, Z), vmem(7, 10, Z), vmem(7, 8, Z),
             vmem(6, X, Z), vmem(6, X, Z), vmem(6, 8, Z), vmem(6, 8, Z),
             vmem(7, X + 2, Z), vmem(7, 8, Z),
             vmem(2, X, Z), vmem(8, Z),
-            vmem(3, X + 4, Z), vmem(3, 10, Z), vmem(ROWS, WIN),
-            vmem(2, 3, ROWS + 2, WIN), vmem(2, 3, 10, WIN),
-            vmem(10, 3, PAD), vmem(10, 2, PAD), vmem(2, 8, Z), vmem(2, 8, WIN),
+            vmem(3, X + 4, Z), vmem(3, 10, Z), vmem(LEVELS, ROWS, WIN),
+            vmem(7, 3, ROWS + 2, WIN), vmem(2, 3, 10, WIN),
+            vmem(10, 3, PAD), vmem(10, 2, PAD), vmem(6, 2, 8, Z), vmem(6, 2, 8, WIN),
             vmem(ROWS, WIN), vmem(ROWS, Z), vmem(ROWS, 8), vmem(2, 7, Z),
             vmem(2, 2, WIN), vmem(2, 4, WIN),
             vmem(2, 8), vmem(2, GROUP, 8), vmem(2, 8), vmem(2, nhi, 8),
-            pltpu.SemaphoreType.DMA((21,)), pltpu.SemaphoreType.DMA((21,)),
+            pltpu.SemaphoreType.DMA((23,)), pltpu.SemaphoreType.DMA((23,)),
             pltpu.SemaphoreType.DMA((2, 2, GROUP)), pltpu.SemaphoreType.DMA((2, 2, GROUP)),
         ],
         compiler_params=pltpu.CompilerParams(

time: 79.5 us -> 71.2 us (0.90)
  the two profiles are of different devices: /device:TPU:0 before, /device:TPU:32 now
where the time goes in v2:
time: 71.2 us; the launch traced here: 71 us
  Pallas kernels  66.9 us (94%)
  between operations  2.4 us (3%)
  local copies, waits for them, and re-layouts  1.67 us (2%)
    pallas_call x1, Pallas kernels, local(): pl.pallas_call(functools.partial(kernel, nx), out_shape=(jax.ShapeDtypeSt...  66.9 us
    unnamed x1, local copies, waits for them, and re-layouts  1.67 us

profile of v2, /device:TPU:32, one launch (start us, length us, event | category | flops | bytes accessed | tf_op | source)
XLA Modules:
  0.0 71.0 jit_solution(17899266772690965990)
XLA Ops:
  0.6 66.9 %shard_map.41 = (f32[512,128]{1,0:T(8,128)}, f32[1,1]{1,0:T(1,128)}) custom-call(f32[512,128]{1,0:T(8,128)} %bitcast.4, f32[512,128]{1,0:T(8,128)} %bitcast.5), custom_call_target="tpu_custom_call" | custom-call | tf_op jit(solution)/shard_map/pallas_call | solution.py:627
  68.2 1.7 %copy.7 = f32[32,16,128]{2,1,0:T(8,128)} copy(f32[32,16,128]{2,1,0:T(8,128)} %bitcast.6) | data formatting | bytes 524288

commit v3 on v2

--- a/solution.py
+++ b/solution.py
@@ -58,6 +58,7 @@
         return 0
     if isinstance(blocks, int) and blocks == 1:
         block(0, 0)
+        return
     else:
         lax.fori_loop(0, blocks, block, 0)
 
@@ -76,8 +77,8 @@
     return jnp.where(k == 0, 7, 8 + lax.rem(k, 2))
 
 
-def kernel(nx, pred_hbm, label_hbm, out, loss, pred, label, in_sem, E, S, M1, M2, SM1, SM2, D, SP, SD, SSP, GB, SGB, SK, SSK,
-           HX, SHX, HZ, G, SG, T, T2, SX, SX2, F, FO, RZ, RX, PS, PR, ARS, AR1, AR2S, AR2,
+def kernel(nx, pred_hbm, label_hbm, out, loss, pred, label, in_sem, E, S, M1, M2, SM1, SM2, D, SP, SD, SSP, GB, SGB, CT, SCT, SK, SSK,
+           HX, SHX, HZ, G, SG, T, T2, SX, SX2, LE, SLE, LM, BM, SLM, SBM, F, FO, RZ, RX, PS, PR, ARS, AR1, AR2S, AR2,
            send_sem, recv_sem, ar_send, ar_recv):
     gz, gx, gy = lax.axis_index("gz"), lax.axis_index("gx"), lax.axis_index("gy")
     prev, nxt = lax.rem(gx + nx - 1, nx), lax.rem(gx + 1, nx)
@@ -202,13 +203,16 @@
                 for f in (0, 1) for k in range(LEVELS + 1) for at in (0, PAD - 8)]
     run(1, 4, 2, strip_rims)
     run(0, 17, 2, lambda r, _, m: [(G, (p, q, r), zero_w) for p in range(LEVELS + 1) for q in range(3)])
-    run(0, 4, 8, lambda r, _, m: [(HZ, (k, r), zero_w) for k in range(LEVELS)])
+    for k in range(LEVELS):
+        HZ[k, 0] = zero_w
     run(0, 2, 5, lambda j, _, m: [(SG, (p, q, j), zero_w) for p in (0, 1) for q in range(3)])
     run(0, 4, 5, lambda i, _, m: [(HX, (q, i), zero_o) for q in range(3)])
     run(0, 4, 4, lambda i, _, m: [(SK, (0, i), zero_o), (SK, (1, i), zero_o), (GB, (LEVELS, i + 1), zero_o)])
     run(0, 1, 8, lambda j, _, m: [(SSK, (j,), zero_o), (SGB, (LEVELS, j), zero_o)])
     for k in range(LEVELS + 1):
         GB[k, 0] = zero_o
+        CT[0] = zero_o
+        CT[X + 1] = zero_o
         GB[k, X + 1] = zero_o
     for q in range(10):
         for p in range(3):
@@ -235,8 +239,11 @@
                 E[7 * f, r, W] = zero_w + 2.0
         RX[0] = jnp.zeros((7, Z, Y), jnp.float32)
 
-    def turn(r):
-        return lax.rem(128 + 111 + 2 * gy - 32 * (r // 8), 128)
+    seam_turn = 111 + 2 * gy
+
+    def place(r):
+        g = lax.div(r, 8)
+        return r - 8 * g, seam_turn - 32 * g
 
     def sides(v, seen):
         lane = lane_of(v)
@@ -290,7 +297,7 @@
         lower, upper = pair(c)
         m = jnp.minimum(jnp.minimum(c, lower), upper)
         m = jnp.minimum(m, jnp.minimum(ref[at + (i, WL)], ref[at + (i, WU)]))
-        return jnp.minimum(m, jnp.minimum(centre(-1), centre(1)))
+        return jnp.minimum(m, jnp.minimum(centre(-1), centre(1))), lower
 
     def depth_max(ref, at, i):
         c = ref[at + (i, O)]
@@ -304,13 +311,16 @@
         blocks = jnp.where(k < 4, 3, 2)
 
         def strip_erode(j, q, memo):
-            return [(S, (f, k + 1, j + 1, W), eroded(S, (f, k), j + 1, q, memo, strip_sides))]
+            m, lower = eroded(S, (f, k), j + 1, q, memo, strip_sides)
+            return [(S, (f, k + 1, j + 1, W), m)] + ([(SLE, (k, j), lower)] if f == 0 else [])
         run(0, 1, 8, strip_erode)
         wrap_strip(S, (f, k + 1), W, 2.0)
 
         def erode(r, q, memo):
-            seen = roll(S[f, k, lax.rem(r, 8) + 1, W], turn(r))
-            return [(E, (slot_of(f, k + 1), r + 1, W), eroded(E, (slot_of(f, k),), r + 1, q, memo, lambda c: sides(c, seen)))]
+            j, by = place(r)
+            seen = roll(S[f, k, j + 1, W], by)
+            m, lower = eroded(E, (slot_of(f, k),), r + 1, q, memo, lambda c: sides(c, seen))
+            return [(E, (slot_of(f, k + 1), r + 1, W), m)] + ([(LE, (k, r), lower)] if f == 0 else [])
         run(start, blocks, 10, erode)
         cap_rows(f, k + 1)
 
@@ -324,9 +334,10 @@
             todo = [(SM2, (slot, j), v)]
             if f == 0:
                 lower, upper = strip_sides(v)
-                delta = jnp.maximum(S[f, k, j + 1, O] - max3(lower, v, upper), 0.0)
+                best = max3(lower, v, upper)
+                delta = jnp.maximum(S[f, k, j + 1, O] - best, 0.0)
                 prior = SSK[j]
-                todo += [(SD, (k, j), delta), (SSP, (k, j), prior),
+                todo += [(SLM, (k, j), lower), (SBM, (k, j), best), (SD, (k, j), delta), (SSP, (k, j), prior),
                          (SSK, (j,), prior + jnp.maximum(delta - prior * delta, 0.0))]
             return todo
         run(0, 1, 8, strip_rows)
@@ -346,12 +357,13 @@
         def rest(i, q, memo):
             v = max3(*[once(memo, q + d, lambda d=d: M1[slot, i + d]) for d in range(3)])
             r = i + 8
-            lower, upper = sides(v, roll(SM2[slot, lax.rem(r, 8)], turn(r)))
-            delta = jnp.maximum(E[slot_of(f, k), r + 1, O] - max3(lower, v, upper), 0.0)
+            lower, upper = sides(v, roll(SM2[slot, q], seam_turn - 4 * (r - q)))
+            best = max3(lower, v, upper)
+            delta = jnp.maximum(E[slot_of(f, k), r + 1, O] - best, 0.0)
             prior = SK[f, i]
             todo = [(M2, (slot, i), v), (SK, (f, i), prior + jnp.maximum(delta - prior * delta, 0.0))]
             if f == 0:
-                todo += [(D, (k, i), delta), (SP, (k, i), prior)]
+                todo += [(D, (k, i), delta), (SP, (k, i), prior), (LM, (k, i), lower), (BM, (k, i), best)]
             return todo
         run(0, 2, 8, rest)
 
@@ -425,12 +437,8 @@
         lax.fori_loop(0, LEVELS, level, 0)
         ar_start(f, f)
 
-    both, alone = ar_end(0)
-    pred_total = alone
-    tprec = (both + 1.0) / (pred_total + 1.0)
-
     def chain(i, _, memo):
-        t = E[7, i + 9, O] - tprec
+        t = zero_o + 1.0
         todo = []
         for k in range(LEVELS - 1, -1, -1):
             delta, prior = D[k, i], SP[k, i]
@@ -441,7 +449,7 @@
     run(0, 4, 4, chain)
 
     def strip_chain(j, _, memo):
-        t = S[1, 0, j + 1, O] - tprec
+        t = zero_o + 1.0
         lane = lane_of(t)
         mine = (lane >= 32) & (lane < 96)
         for k in range(LEVELS - 1, -1, -1):
@@ -452,6 +460,13 @@
         return []
     run(0, 2, 4, strip_chain)
 
+    both, alone = ar_end(0)
+    pred_total = alone
+    tprec = (both + 1.0) / (pred_total + 1.0)
+
+    run(0, 2, 8, lambda i, _, m: [(CT, (i + 1,), E[7, i + 9, O] - tprec)])
+    run(0, 1, 8, lambda j, _, m: [(SCT, (j,), S[1, 0, j + 1, O] - tprec)])
+
     def strip_back(step, _):
         k = LEVELS - 1 - step
         old = lax.rem(step, 2)
@@ -459,9 +474,8 @@
 
         def strip_cols(j, _, memo):
             a = SM2[k, j]
-            lower, upper = strip_sides(a)
-            gc, gl, gu = route(-SGB[k, j], max3(lower, a, upper), (a, lower))
-            todo = [(SX, (k, 0, j), gl), (SX, (k, 1, j), gu)]
+            gc, gl, gu = route(-SGB[k, j] * SCT[j], SBM[k, j], (a, SLM[k, j]))
+            todo = [(SX, (k, j), jnp.where(gy == 0, gl, gu))]
             g = gc + roll(gl, 127) + roll(gu, 1)
             gc, gl, gu = route(g, a, (SM1[k, j + 1], SM1[k, j]))
             return todo + [(SHX, (0, j + 1), gc), (SHX, (1, j + 1), gl), (SHX, (2, j + 1), gu)]
@@ -472,19 +486,18 @@
         def strip_depth(j, q, memo):
             g = SHX[0, j + 1] + SHX[1, j + 2] + SHX[2, j]
             gc, gl, gu = route(g, SM1[k, j + 1], (S[0, k + 1, j + 1, O], S[0, k + 1, j + 1, OL]))
-            T[q, 0, O] = gc + SGB[k + 1, j]
+            T[q, 0, O] = gc + SGB[k + 1, j] * SCT[j]
             T[q, 1, O] = gl
             T[q, 2, O] = gu
             g = SG[old, 0, j + 1] + SG[old, 1, j + 2] + SG[old, 2, j]
             g = g + T[q, 0, W] + T[q, 1, WU] + T[q, 2, WL]
             c = S[0, k, j + 1, W]
-            lower, upper = strip_sides(c)
             gc, zl, zu, xl, xu, yl, yu = route(
                 g, S[0, k + 1, j + 1, W],
-                (c, S[0, k, j + 1, WL], S[0, k, j + 1, WU], S[0, k, j, W], S[0, k, j + 2, W], lower))
+                (c, S[0, k, j + 1, WL], S[0, k, j + 1, WU], S[0, k, j, W], S[0, k, j + 2, W], SLE[k, j]))
             T2[q, 0, W] = zl
             T2[q, 1, W] = zu
-            return [(SX2, (k, 0, j), yl), (SX2, (k, 1, j), yu),
+            return [(SX2, (k, j), jnp.where(gy == 0, yl, yu)),
                     (SG, (new, 0, j + 1), gc + roll(yl, 127) + roll(yu, 1) + T2[q, 0, WU] + T2[q, 1, WL]),
                     (SG, (new, 1, j + 1), xl), (SG, (new, 2, j + 1), xu)]
         run(0, 2, 4, strip_depth)
@@ -493,44 +506,50 @@
         return 0
     lax.fori_loop(0, LEVELS, strip_back, 0)
 
-    def open_back(k, _):
-        def cols(i, _, memo):
-            a = M2[k, i]
-            r = i + 8
-            by, j = turn(r), lax.rem(r, 8)
-            lower, upper = sides(a, roll(SM2[k, j], by))
-            gc, gl, gu = route(-GB[k, i + 1], max3(lower, a, upper), (a, lower))
-            g = gc + gather_sides(gl, gu, roll(SX[k, gy, j], by))
-            gc, gl, gu = route(g, a, (M1[k, i + 1], M1[k, i]))
-            return [(HX, (0, i + 2), gc), (HX, (1, i + 2), gl), (HX, (2, i + 2), gu)]
-        run(0, 2, 8, cols)
-
-        def depths(i, q, memo):
-            g = HX[0, i + 1] + HX[1, i + 2] + HX[2, i]
-            gc, gl, gu = route(g, M1[k, i], (E[k + 1, i + 8, O], E[k + 1, i + 8, OL]))
-            T[q, 0, O] = gc + GB[k + 1, i]
-            T[q, 1, O] = gl
-            T[q, 2, O] = gu
-            return [(HZ, (k, i + 7), T[q, 0, W] + T[q, 1, WU] + T[q, 2, WL])]
-        run(0, 3, 6, depths)
-
-        @pl.when(k == 2)
-        def _():
-            ar_middle(1)
+    def open_cols(k, i, j, g):
+        a = M2[k, i]
+        by = seam_turn - 32 * g
+        gc, gl, gu = route(-GB[k, i + 1] * CT[i + 1], BM[k, i], (a, LM[k, i]))
+        g = gc + gather_sides(gl, gu, roll(SX[k, j], by))
+        gc, gl, gu = route(g, a, (M1[k, i + 1], M1[k, i]))
+        return [(HX, (0, i + 2), gc), (HX, (1, i + 2), gl), (HX, (2, i + 2), gu)]
+
+    def open_depths(k, i, q):
+        g = HX[0, i + 1] + HX[1, i + 2] + HX[2, i]
+        gc, gl, gu = route(g, M1[k, i], (E[k + 1, i + 8, O], E[k + 1, i + 8, OL]))
+        T[q, 0, O] = gc + GB[k + 1, i] * CT[i]
+        T[q, 1, O] = gl
+        T[q, 2, O] = gu
+        return [(HZ, (k, i + 1), T[q, 0, W] + T[q, 1, WU] + T[q, 2, WL])]
+
+    def open_all(k, _):
+        lax.fori_loop(0, 2, lambda b, c: run(8 * b, 1, 8, lambda i, q, memo: open_cols(k, i, q, b + 1)) or 0, 0)
+        run(0, 3, 6, lambda i, q, memo: open_depths(k, i, q))
         return 0
-    lax.fori_loop(0, LEVELS, open_back, 0)
+
+    def open_outer(k, _):
+        lax.fori_loop(0, 2, lambda b, c: run(12 * b, 1, 4, lambda i, q, memo: open_cols(k, i, 4 * b + q, b + 1)) or 0, 0)
+        run(lambda b: 14 * b, 2, 4, lambda i, q, memo: open_depths(k, i, q))
+        return 0
+
+    def open_inner(k):
+        lax.fori_loop(0, 2, lambda b, c: run(8 * b, 1, 8, lambda i, q, memo: open_cols(k, i, q, b + 1)) or 0, 0)
+        run(4, 2, 5, lambda i, q, memo: open_depths(k, i, q))
+
+    lax.fori_loop(3, LEVELS, open_all, 0)
+    ar_middle(1)
+    lax.fori_loop(0, 3, open_outer, 0)
 
     def erode_back(k, r, q, memo):
-        g = G[k + 1, 0, r + 1] + G[k + 1, 1, r + 2] + G[k + 1, 2, r] + HZ[k, r]
-        by, j = turn(r), lax.rem(r, 8)
+        g = G[k + 1, 0, r + 1] + G[k + 1, 1, r + 2] + G[k + 1, 2, r] + HZ[k, jnp.where((r > 6) & (r < 25), r - 6, 0)]
+        j, by = place(r)
         under, c, over = [once(memo, q + d, lambda d=d: E[k, r + d, W]) for d in range(3)]
-        lower, upper = sides(c, roll(S[0, k, j + 1, W], by))
         gc, zl, zu, xl, xu, yl, yu = route(
             g, E[k + 1, r + 1, W],
-            (c, E[k, r + 1, WL], E[k, r + 1, WU], under, over, lower))
+            (c, E[k, r + 1, WL], E[k, r + 1, WU], under, over, LE[k, r]))
         T2[q, 0, W] = zl
         T2[q, 1, W] = zu
-        return [(G, (k, 0, r + 1), gc + gather_sides(yl, yu, roll(SX2[k, gy, j], by)) + T2[q, 0, WU] + T2[q, 1, WL]),
+        return [(G, (k, 0, r + 1), gc + gather_sides(yl, yu, roll(SX2[k, j], by)) + T2[q, 0, WU] + T2[q, 1, WL]),
                 (G, (k, 1, r + 1), xl), (G, (k, 2, r + 1), xu)]
 
     def outer(step, _):
@@ -574,6 +593,10 @@
     def inside(step, _):
         k = LEVELS - 1 - step
         at = (k + 1) // 2
+
+        @pl.when(k < 3)
+        def _():
+            open_inner(k)
         run(8 + 2 * at, 4 - at, 4, lambda r, q, memo: erode_back(k, r, q, memo))
 
         @pl.when(step == 1)
@@ -604,11 +627,11 @@
         copy.wait_recv()
 
     def give(x, _, memo, extra):
-        g = FO[x + 8] + GB[0, x + 1]
+        g = FO[x + 8] + GB[0, x + 1] * CT[x + 1]
         if extra is not None:
             g = g + extra(x)
         g = g * by_prec + SK[1, x] * by_sens
-        return [(out, (pl.ds(x + X * 8 * t, 8, stride=X), slice(None)), g[8 * t:8 * t + 8]) for t in range(Z // 8)]
+        return [(out, (x,), g)]
     run(0, 1, 7, functools.partial(give, extra=lambda x: RX[1, x]))
     run(7, 1, 2, functools.partial(give, extra=None))
     run(9, 1, 7, functools.partial(give, extra=lambda x: RX[0, x - 9]))
@@ -626,7 +649,7 @@
 
     grad, loss = pl.pallas_call(
         functools.partial(kernel, nx),
-        out_shape=(jax.ShapeDtypeStruct((Z * X, Y), f32), jax.ShapeDtypeStruct((1, 1), f32)),
+        out_shape=(jax.ShapeDtypeStruct((X, Z, Y), f32), jax.ShapeDtypeStruct((1, 1), f32)),
         in_specs=[pl.BlockSpec(memory_space=pl.ANY)] * 2,
         out_specs=[pl.BlockSpec(memory_space=pltpu.VMEM)] * 2,
         scratch_shapes=[
@@ -634,11 +657,13 @@
             vmem(10, ROWS + 2, PAD), vmem(2, 7, 10, PAD),
             vmem(7, X + 2, Z), vmem(7, X, Z), vmem(7, 10, Z), vmem(7, 8, Z),
             vmem(6, X, Z), vmem(6, X, Z), vmem(6, 8, Z), vmem(6, 8, Z),
-            vmem(7, X + 2, Z), vmem(7, 8, Z),
+            vmem(7, X + 2, Z), vmem(7, 8, Z), vmem(X + 2, Z), vmem(8, Z),
             vmem(2, X, Z), vmem(8, Z),
-            vmem(3, X + 4, Z), vmem(3, 10, Z), vmem(LEVELS, ROWS, WIN),
+            vmem(3, X + 4, Z), vmem(3, 10, Z), vmem(LEVELS, X + 3, WIN),
             vmem(7, 3, ROWS + 2, WIN), vmem(2, 3, 10, WIN),
-            vmem(10, 3, PAD), vmem(10, 2, PAD), vmem(6, 2, 8, Z), vmem(6, 2, 8, WIN),
+            vmem(10, 3, PAD), vmem(10, 2, PAD), vmem(6, 8, Z), vmem(6, 8, WIN),
+            vmem(6, ROWS, WIN), vmem(6, 8, WIN),
+            vmem(6, X, Z), vmem(6, X, Z), vmem(6, 8, Z), vmem(6, 8, Z),
             vmem(ROWS, WIN), vmem(ROWS, Z), vmem(ROWS, 8), vmem(2, 7, Z),
             vmem(2, 2, WIN), vmem(2, 4, WIN),
             vmem(2, 8), vmem(2, GROUP, 8), vmem(2, 8), vmem(2, nhi, 8),
@@ -646,9 +671,9 @@
             pltpu.SemaphoreType.DMA((2, 2, GROUP)), pltpu.SemaphoreType.DMA((2, 2, GROUP)),
         ],
         compiler_params=pltpu.CompilerParams(
-            collective_id=0, has_side_effects=True, vmem_limit_bytes=56 * 1024 * 1024),
+            collective_id=0, has_side_effects=True, vmem_limit_bytes=62 * 1024 * 1024),
     )(prediction.reshape(Z * X, Y), label.reshape(Z * X, Y))
-    return loss.reshape(()), grad.reshape(Z, X, Y)
+    return loss.reshape(()), jnp.transpose(grad, (1, 0, 2))
 
 
 def solution(mesh):

time: 71.2 us -> 63.9 us (0.90)
  Pallas kernels: 66.9 us -> 59.5 us
    pallas_call x1, Pallas kernels: 66.9 us -> 59.5 us  [local(): pl.pallas_call(functools.partial(kernel, nx), out_shape=(jax.ShapeDtypeSt...]
where the time goes in v3:
time: 63.9 us; the launch traced here: 63.7 us
  Pallas kernels  59.5 us (93%)
  between operations  2.4 us (4%)
  local copies, waits for them, and re-layouts  1.81 us (3%)
    pallas_call x1, Pallas kernels, local(): pl.pallas_call(functools.partial(kernel, nx), out_shape=(jax.ShapeDtypeSt...  59.5 us
    unnamed x1, local copies, waits for them, and re-layouts  1.81 us

profile of v3, /device:TPU:32, one launch (start us, length us, event | category | flops | bytes accessed | tf_op | source)
XLA Modules:
  0.0 63.7 jit_solution(4271756817410470929)
XLA Ops:
  0.6 59.5 %shard_map.41 = (f32[16,32,128]{2,1,0:T(8,128)}, f32[1,1]{1,0:T(1,128)}) custom-call(f32[512,128]{1,0:T(8,128)} %bitcast.4, f32[512,128]{1,0:T(8,128)} %bitcast.5), custom_call_target="tpu_custom_call" | custom-call | tf_op jit(solution)/shard_map/pallas_call | solution.py:650
  60.1 1.8 %copy.4 = f32[32,16,128]{2,1,0:T(8,128)} copy(f32[32,16,128]{2,0,1:T(8,128)} %bitcast.6) | data formatting | bytes 524288

commit v4 on v3

--- a/solution.py
+++ b/solution.py
@@ -96,6 +96,11 @@
     def member(i):
         return (i // (2 * LO), hi * LO + lax.rem(i // 2, LO), lax.rem(i, 2))
 
+    loads = [pltpu.make_async_copy(src, dst, in_sem.at[f])
+             for f, (src, dst) in enumerate(((pred_hbm, pred), (label_hbm, label)))]
+    for load in loads:
+        load.start()
+
     barrier = pltpu.get_barrier_semaphore()
     has_prev, has_nxt = gx > 0, gx < nx - 1
     for inside, row in ((has_prev, prev), (has_nxt, nxt)):
@@ -108,19 +113,16 @@
     for device in greet:
         pl.semaphore_signal(barrier, inc=1, device_id=device, device_id_type=MESH)
 
-    loads = [pltpu.make_async_copy(src, dst, in_sem.at[f])
-             for f, (src, dst) in enumerate(((pred_hbm, pred), (label_hbm, label)))]
-    for load in loads:
-        load.start()
-
-    for f, ref in ((0, pred), (1, label)):
+    def lay_out(f):
+        ref = (pred, label)[f]
         loads[f].wait()
 
-        def bring(x, _, memo, f=f, ref=ref):
+        def bring(x, _, memo):
             return [(E, (7 * f, 9 + x, pl.ds(o + 8 * t, 8)), ref[pl.ds(x + X * 8 * t, 8, stride=X), :])
                     for t in range(Z // 8)]
         run(0, 2, 8, bring)
 
+    lay_out(0)
     zero_w = jnp.zeros((WIN, Y), jnp.float32)
     zero_o = jnp.zeros((Z, Y), jnp.float32)
     pl.semaphore_wait(barrier, len(greet) + jnp.where(has_prev, 2, 0) + jnp.where(has_nxt, 2, 0))
@@ -188,6 +190,7 @@
             send(8 * f + 7, PS.at[f, 1], PR.at[f, 0], (gz, nxt, 1 - gy), 1)]
 
     depth = first_halos(0)
+    lay_out(1)
     second_halos(0, depth)
     depth = first_halos(1)
     second_halos(1, depth)
@@ -214,7 +217,7 @@
         CT[0] = zero_o
         CT[X + 1] = zero_o
         GB[k, X + 1] = zero_o
-    for q in range(10):
+    for q in range(8):
         for p in range(3):
             T[q, p] = jnp.zeros((PAD, Y), jnp.float32)
         for p in range(2):
@@ -306,10 +309,7 @@
         upper = jnp.where(plane == zhigh, c, ref[at + (i, OU)])
         return max3(lower, c, upper)
 
-    def level_forward(f, k, slot):
-        start = jnp.where(k < 4, 1, 6)
-        blocks = jnp.where(k < 4, 3, 2)
-
+    def level_forward(f, k, slot, first, rows):
         def strip_erode(j, q, memo):
             m, lower = eroded(S, (f, k), j + 1, q, memo, strip_sides)
             return [(S, (f, k + 1, j + 1, W), m)] + ([(SLE, (k, j), lower)] if f == 0 else [])
@@ -317,12 +317,13 @@
         wrap_strip(S, (f, k + 1), W, 2.0)
 
         def erode(r, q, memo):
-            j, by = place(r)
-            seen = roll(S[f, k, j + 1, W], by)
+            j, g = r % 8, r // 8
+            seen = roll(S[f, k, j + 1, W], seam_turn - 32 * g)
             m, lower = eroded(E, (slot_of(f, k),), r + 1, q, memo, lambda c: sides(c, seen))
+            if r in (7, 24):
+                m = jnp.where(gx == (0 if r == 7 else nx - 1), zero_w + 2.0, m)
             return [(E, (slot_of(f, k + 1), r + 1, W), m)] + ([(LE, (k, r), lower)] if f == 0 else [])
-        run(start, blocks, 10, erode)
-        cap_rows(f, k + 1)
+        run(first, 1, rows, erode)
 
         def strip_depth(j, _, memo):
             return [(SM1, (slot, j + 1), depth_max(S, (f, k + 1), j + 1))]
@@ -343,21 +344,16 @@
         run(0, 1, 8, strip_rows)
 
         def depth_rows(i, _, memo):
-            return [(M1, (slot, i), depth_max(E, (slot_of(f, k + 1),), i + 8))]
-        run(0, 2, 9, depth_rows)
-
-        @pl.when(gx == 0)
-        def _():
-            M1[slot, 0] = zero_o
-
-        @pl.when(gx == nx - 1)
-        def _():
-            M1[slot, X + 1] = zero_o
+            m = depth_max(E, (slot_of(f, k + 1),), i + 8)
+            if i in (0, X + 1):
+                m = jnp.where(gx == (0 if i == 0 else nx - 1), zero_o, m)
+            return [(M1, (slot, i), m)]
+        run(0, 1, X + 2, depth_rows)
 
         def rest(i, q, memo):
             v = max3(*[once(memo, q + d, lambda d=d: M1[slot, i + d]) for d in range(3)])
             r = i + 8
-            lower, upper = sides(v, roll(SM2[slot, q], seam_turn - 4 * (r - q)))
+            lower, upper = sides(v, roll(SM2[slot, i % 8], seam_turn - 32 * (r // 8)))
             best = max3(lower, v, upper)
             delta = jnp.maximum(E[slot_of(f, k), r + 1, O] - best, 0.0)
             prior = SK[f, i]
@@ -365,7 +361,7 @@
             if f == 0:
                 todo += [(D, (k, i), delta), (SP, (k, i), prior), (LM, (k, i), lower), (BM, (k, i), best)]
             return todo
-        run(0, 2, 8, rest)
+        run(0, 1, X, rest)
 
     def ar_copy(n, phase, slot, src, dst, number, device):
         return pltpu.make_async_remote_copy(
@@ -427,14 +423,15 @@
         cap_rows(f, 0)
         build_strip(f)
 
-        def level(k, _, f=f):
-            level_forward(f, k, k if f == 0 else LEVELS)
-            if f == 1:
+        def level(first, rows, k, f=f):
+            level_forward(f, k, k if f == 0 else LEVELS, first, rows)
+            if f == 1 and rows == 28:
                 @pl.when(k == 2)
                 def _():
                     ar_middle(0)
             return 0
-        lax.fori_loop(0, LEVELS, level, 0)
+        lax.fori_loop(0, 4, lambda k, _: level(2, 28, k), 0)
+        lax.fori_loop(4, LEVELS, lambda k, _: level(6, 20, k), 0)
         ar_start(f, f)
 
     def chain(i, _, memo):
@@ -500,7 +497,7 @@
             return [(SX2, (k, j), jnp.where(gy == 0, yl, yu)),
                     (SG, (new, 0, j + 1), gc + roll(yl, 127) + roll(yu, 1) + T2[q, 0, WU] + T2[q, 1, WL]),
                     (SG, (new, 1, j + 1), xl), (SG, (new, 2, j + 1), xu)]
-        run(0, 2, 4, strip_depth)
+        run(0, 1, 8, strip_depth)
         SG[new, 1, 9] = roll(SG[new, 1, 1], 96)
         SG[new, 2, 0] = roll(SG[new, 2, 8], 32)
         return 0
@@ -554,7 +551,7 @@
 
     def outer(step, _):
         k = LEVELS - 1 - step
-        run(lambda b: jnp.where(b < 2, 1 + k + 4 * b, 15 - k + 4 * b), 4, 4, lambda r, q, memo: erode_back(k, r, q, memo))
+        run(lambda b: jnp.where(b == 0, 2 + k, 23 - k), 2, 7, lambda r, q, memo: erode_back(k, r, q, memo))
         return 0
     lax.fori_loop(0, LEVELS, outer, 0)
 
@@ -661,7 +658,7 @@
             vmem(2, X, Z), vmem(8, Z),
             vmem(3, X + 4, Z), vmem(3, 10, Z), vmem(LEVELS, X + 3, WIN),
             vmem(7, 3, ROWS + 2, WIN), vmem(2, 3, 10, WIN),
-            vmem(10, 3, PAD), vmem(10, 2, PAD), vmem(6, 8, Z), vmem(6, 8, WIN),
+            vmem(8, 3, PAD), vmem(8, 2, PAD), vmem(6, 8, Z), vmem(6, 8, WIN),
             vmem(6, ROWS, WIN), vmem(6, 8, WIN),
             vmem(6, X, Z), vmem(6, X, Z), vmem(6, 8, Z), vmem(6, 8, Z),
             vmem(ROWS, WIN), vmem(ROWS, Z), vmem(ROWS, 8), vmem(2, 7, Z),

time: 63.9 us -> 59.1 us (0.925)
  Pallas kernels: 59.5 us -> 54.7 us
    pallas_call x1, Pallas kernels: 59.5 us -> 54.7 us  [local(): pl.pallas_call(functools.partial(kernel, nx), out_shape=(jax.ShapeDtypeSt...]
where the time goes in v4:
time: 59.1 us; the launch traced here: 58.9 us
  Pallas kernels  54.7 us (93%)
  between operations  2.4 us (4%)
  local copies, waits for them, and re-layouts  1.81 us (3%)
    pallas_call x1, Pallas kernels, local(): pl.pallas_call(functools.partial(kernel, nx), out_shape=(jax.ShapeDtypeSt...  54.7 us
    unnamed x1, local copies, waits for them, and re-layouts  1.81 us

profile of v4, /device:TPU:32, one launch (start us, length us, event | category | flops | bytes accessed | tf_op | source)
XLA Modules:
  0.0 58.9 jit_solution(10181632177875363257)
XLA Ops:
  0.6 54.7 %shard_map.41 = (f32[16,32,128]{2,1,0:T(8,128)}, f32[1,1]{1,0:T(1,128)}) custom-call(f32[512,128]{1,0:T(8,128)} %bitcast.4, f32[512,128]{1,0:T(8,128)} %bitcast.5), custom_call_target="tpu_custom_call" | custom-call | tf_op jit(solution)/shard_map/pallas_call | solution.py:647
  55.3 1.8 %copy.4 = f32[32,16,128]{2,1,0:T(8,128)} copy(f32[32,16,128]{2,0,1:T(8,128)} %bitcast.6) | data formatting | bytes 524288

commit v5 on v4

--- a/solution.py
+++ b/solution.py
@@ -12,8 +12,8 @@
 WIN = Z + 8
 PAD = WIN + 16
 ROWS = X + 16
-GROUP = 16
-LO = 4
+GROUP = 8
+LO = 2
 SEMS = 64
 MESH = pl.DeviceIdType.MESH
 
@@ -41,8 +41,9 @@
     parts = []
     for value in candidates:
         hit = value == best
-        parts.append(jnp.where(hit, g, zero))
-        g = jnp.where(hit, zero, g)
+        part = jnp.where(hit, g, zero)
+        parts.append(part)
+        g = g - part
     parts.append(g)
     return parts
 
@@ -77,7 +78,7 @@
     return jnp.where(k == 0, 7, 8 + lax.rem(k, 2))
 
 
-def kernel(nx, pred_hbm, label_hbm, out, loss, pred, label, in_sem, E, S, M1, M2, SM1, SM2, D, SP, SD, SSP, GB, SGB, CT, SCT, SK, SSK,
+def kernel(nx, pred_hbm, label_hbm, out, loss, pred, label, in_sem, E, S, M1, M2, SM1, SM2, SP, SSP, GB, SGB, CT, SCT, SK, SSK,
            HX, SHX, HZ, G, SG, T, T2, SX, SX2, LE, SLE, LM, BM, SLM, SBM, F, FO, RZ, RX, PS, PR, ARS, AR1, AR2S, AR2,
            send_sem, recv_sem, ar_send, ar_recv):
     gz, gx, gy = lax.axis_index("gz"), lax.axis_index("gx"), lax.axis_index("gy")
@@ -220,6 +221,7 @@
     for q in range(8):
         for p in range(3):
             T[q, p] = jnp.zeros((PAD, Y), jnp.float32)
+    for q in range(8):
         for p in range(2):
             T2[q, p] = jnp.zeros((PAD, Y), jnp.float32)
     for r in (0, 1, ROWS, ROWS + 1):
@@ -338,7 +340,7 @@
                 best = max3(lower, v, upper)
                 delta = jnp.maximum(S[f, k, j + 1, O] - best, 0.0)
                 prior = SSK[j]
-                todo += [(SLM, (k, j), lower), (SBM, (k, j), best), (SD, (k, j), delta), (SSP, (k, j), prior),
+                todo += [(SLM, (k, j), lower), (SBM, (k, j), best), (SGB, (k, j), delta), (SSP, (k, j), prior),
                          (SSK, (j,), prior + jnp.maximum(delta - prior * delta, 0.0))]
             return todo
         run(0, 1, 8, strip_rows)
@@ -357,9 +359,9 @@
             best = max3(lower, v, upper)
             delta = jnp.maximum(E[slot_of(f, k), r + 1, O] - best, 0.0)
             prior = SK[f, i]
-            todo = [(M2, (slot, i), v), (SK, (f, i), prior + jnp.maximum(delta - prior * delta, 0.0))]
+            todo = [(SK, (f, i), prior + jnp.maximum(delta - prior * delta, 0.0))]
             if f == 0:
-                todo += [(D, (k, i), delta), (SP, (k, i), prior), (LM, (k, i), lower), (BM, (k, i), best)]
+                todo += [(M2, (k, i), v), (GB, (k, i + 1), delta), (SP, (k, i), prior), (LM, (k, i), lower), (BM, (k, i), best)]
             return todo
         run(0, 1, X, rest)
 
@@ -438,7 +440,7 @@
         t = zero_o + 1.0
         todo = []
         for k in range(LEVELS - 1, -1, -1):
-            delta, prior = D[k, i], SP[k, i]
+            delta, prior = GB[k, i + 1], SP[k, i]
             on = delta - prior * delta > 0
             GB[k, i + 1] = jnp.where(on, t * (1.0 - prior), 0.0)
             t = jnp.where(on, t * (1.0 - delta), t)
@@ -450,7 +452,7 @@
         lane = lane_of(t)
         mine = (lane >= 32) & (lane < 96)
         for k in range(LEVELS - 1, -1, -1):
-            delta, prior = SD[k, j], SSP[k, j]
+            delta, prior = SGB[k, j], SSP[k, j]
             on = delta - prior * delta > 0
             SGB[k, j] = jnp.where(on & mine, t * (1.0 - prior), 0.0)
             t = jnp.where(on, t * (1.0 - delta), t)
@@ -501,7 +503,6 @@
         SG[new, 1, 9] = roll(SG[new, 1, 1], 96)
         SG[new, 2, 0] = roll(SG[new, 2, 8], 32)
         return 0
-    lax.fori_loop(0, LEVELS, strip_back, 0)
 
     def open_cols(k, i, j, g):
         a = M2[k, i]
@@ -520,22 +521,24 @@
         return [(HZ, (k, i + 1), T[q, 0, W] + T[q, 1, WU] + T[q, 2, WL])]
 
     def open_all(k, _):
-        lax.fori_loop(0, 2, lambda b, c: run(8 * b, 1, 8, lambda i, q, memo: open_cols(k, i, q, b + 1)) or 0, 0)
-        run(0, 3, 6, lambda i, q, memo: open_depths(k, i, q))
+        run(0, 1, X, lambda i, q, memo: open_cols(k, i, i % 8, i // 8 + 1))
+        run(0, 1, X + 2, lambda i, q, memo: open_depths(k, i, q % 8))
         return 0
 
     def open_outer(k, _):
-        lax.fori_loop(0, 2, lambda b, c: run(12 * b, 1, 4, lambda i, q, memo: open_cols(k, i, 4 * b + q, b + 1)) or 0, 0)
-        run(lambda b: 14 * b, 2, 4, lambda i, q, memo: open_depths(k, i, q))
+        for start in (0, 12):
+            run(start, 1, 4, lambda i, q, memo: open_cols(k, i, i % 8, i // 8 + 1))
+        for start in (0, 14):
+            run(start, 1, 4, lambda i, q, memo: open_depths(k, i, start // 14 * 4 + q))
         return 0
 
     def open_inner(k):
-        lax.fori_loop(0, 2, lambda b, c: run(8 * b, 1, 8, lambda i, q, memo: open_cols(k, i, q, b + 1)) or 0, 0)
-        run(4, 2, 5, lambda i, q, memo: open_depths(k, i, q))
-
-    lax.fori_loop(3, LEVELS, open_all, 0)
+        run(2, 1, 12, lambda i, q, memo: open_cols(k, i, i % 8, i // 8 + 1))
+        run(4, 1, 10, lambda i, q, memo: open_depths(k, i, q % 8))
+
+    lax.fori_loop(0, 3, lambda step, _: strip_back(step, 0) + open_all(LEVELS - 1 - step, 0), 0)
     ar_middle(1)
-    lax.fori_loop(0, 3, open_outer, 0)
+    lax.fori_loop(3, LEVELS, lambda step, _: strip_back(step, 0) + open_outer(LEVELS - 1 - step, 0), 0)
 
     def erode_back(k, r, q, memo):
         g = G[k + 1, 0, r + 1] + G[k + 1, 1, r + 2] + G[k + 1, 2, r] + HZ[k, jnp.where((r > 6) & (r < 25), r - 6, 0)]
@@ -652,8 +655,8 @@
         scratch_shapes=[
             vmem(Z * X), vmem(Z * X), pltpu.SemaphoreType.DMA((2,)),
             vmem(10, ROWS + 2, PAD), vmem(2, 7, 10, PAD),
-            vmem(7, X + 2, Z), vmem(7, X, Z), vmem(7, 10, Z), vmem(7, 8, Z),
-            vmem(6, X, Z), vmem(6, X, Z), vmem(6, 8, Z), vmem(6, 8, Z),
+            vmem(7, X + 2, Z), vmem(6, X, Z), vmem(7, 10, Z), vmem(7, 8, Z),
+            vmem(6, X, Z), vmem(6, 8, Z),
             vmem(7, X + 2, Z), vmem(7, 8, Z), vmem(X + 2, Z), vmem(8, Z),
             vmem(2, X, Z), vmem(8, Z),
             vmem(3, X + 4, Z), vmem(3, 10, Z), vmem(LEVELS, X + 3, WIN),
@@ -665,7 +668,7 @@
             vmem(2, 2, WIN), vmem(2, 4, WIN),
             vmem(2, 8), vmem(2, GROUP, 8), vmem(2, 8), vmem(2, nhi, 8),
             pltpu.SemaphoreType.DMA((23,)), pltpu.SemaphoreType.DMA((23,)),
-            pltpu.SemaphoreType.DMA((2, 2, GROUP)), pltpu.SemaphoreType.DMA((2, 2, GROUP)),
+            pltpu.SemaphoreType.DMA((2, 2, max(GROUP, nhi))), pltpu.SemaphoreType.DMA((2, 2, max(GROUP, nhi))),
         ],
         compiler_params=pltpu.CompilerParams(
             collective_id=0, has_side_effects=True, vmem_limit_bytes=62 * 1024 * 1024),

time: 59.1 us -> 57.2 us (0.968)
  Pallas kernels: 54.7 us -> 52.9 us
    pallas_call x1, Pallas kernels: 54.7 us -> 52.9 us  [local(): pl.pallas_call(functools.partial(kernel, nx), out_shape=(jax.ShapeDtypeSt...]
where the time goes in v5:
time: 57.2 us; the launch traced here: 57.1 us
  Pallas kernels  52.9 us (92%)
  between operations  2.4 us (4%)
  local copies, waits for them, and re-layouts  1.81 us (3%)
    pallas_call x1, Pallas kernels, local(): pl.pallas_call(functools.partial(kernel, nx), out_shape=(jax.ShapeDtypeSt...  52.9 us
    unnamed x1, local copies, waits for them, and re-layouts  1.81 us

profile of v5, /device:TPU:32, one launch (start us, length us, event | category | flops | bytes accessed | tf_op | source)
XLA Modules:
  0.0 57.1 jit_solution(1312295183681801720)
XLA Ops:
  0.6 52.9 %shard_map.41 = (f32[16,32,128]{2,1,0:T(8,128)}, f32[1,1]{1,0:T(1,128)}) custom-call(f32[512,128]{1,0:T(8,128)} %bitcast.4, f32[512,128]{1,0:T(8,128)} %bitcast.5), custom_call_target="tpu_custom_call" | custom-call | tf_op jit(solution)/shard_map/pallas_call | solution.py:650
  53.5 1.8 %copy.4 = f32[32,16,128]{2,1,0:T(8,128)} copy(f32[32,16,128]{2,0,1:T(8,128)} %bitcast.6) | data formatting | bytes 524288

commit v6 on v5

--- a/solution.py
+++ b/solution.py
@@ -97,7 +97,7 @@
     def member(i):
         return (i // (2 * LO), hi * LO + lax.rem(i // 2, LO), lax.rem(i, 2))
 
-    loads = [pltpu.make_async_copy(src, dst, in_sem.at[f])
+    loads = [pltpu.make_async_copy(src, dst.at[pl.ds(0, Z * X)], in_sem.at[f])
              for f, (src, dst) in enumerate(((pred_hbm, pred), (label_hbm, label)))]
     for load in loads:
         load.start()
@@ -653,7 +653,7 @@
         in_specs=[pl.BlockSpec(memory_space=pl.ANY)] * 2,
         out_specs=[pl.BlockSpec(memory_space=pltpu.VMEM)] * 2,
         scratch_shapes=[
-            vmem(Z * X), vmem(Z * X), pltpu.SemaphoreType.DMA((2,)),
+            vmem(Z * X + 256), vmem(Z * X + 256), pltpu.SemaphoreType.DMA((2,)),
             vmem(10, ROWS + 2, PAD), vmem(2, 7, 10, PAD),
             vmem(7, X + 2, Z), vmem(6, X, Z), vmem(7, 10, Z), vmem(7, 8, Z),
             vmem(6, X, Z), vmem(6, 8, Z),

time: 57.2 us -> 57.2 us (level)
  no operation moved by 1% of the time
where the time goes in v6:
time: 57.2 us; the launch traced here: 57.1 us
  Pallas kernels  52.9 us (92%)
  between operations  2.4 us (4%)
  local copies, waits for them, and re-layouts  1.81 us (3%)
    pallas_call x1, Pallas kernels, local(): pl.pallas_call(functools.partial(kernel, nx), out_shape=(jax.ShapeDtypeSt...  52.9 us
    unnamed x1, local copies, waits for them, and re-layouts  1.81 us

profile of v6, /device:TPU:32, one launch (start us, length us, event | category | flops | bytes accessed | tf_op | source)
XLA Modules:
  0.0 57.1 jit_solution(13962566593390200739)
XLA Ops:
  0.6 52.9 %shard_map.41 = (f32[16,32,128]{2,1,0:T(8,128)}, f32[1,1]{1,0:T(1,128)}) custom-call(f32[512,128]{1,0:T(8,128)} %bitcast.4, f32[512,128]{1,0:T(8,128)} %bitcast.5), custom_call_target="tpu_custom_call" | custom-call | tf_op jit(solution)/shard_map/pallas_call | solution.py:650
  53.5 1.8 %copy.4 = f32[32,16,128]{2,1,0:T(8,128)} copy(f32[32,16,128]{2,0,1:T(8,128)} %bitcast.6) | data formatting | bytes 524288

commit v7 on v6

--- a/solution.py
+++ b/solution.py
@@ -428,7 +428,7 @@
         def level(first, rows, k, f=f):
             level_forward(f, k, k if f == 0 else LEVELS, first, rows)
             if f == 1 and rows == 28:
-                @pl.when(k == 2)
+                @pl.when(k == 1)
                 def _():
                     ar_middle(0)
             return 0
@@ -575,20 +575,18 @@
     def own_planes(r, _, memo):
         return [(FO, (r,), F[r, pl.ds(mine, Z)])]
 
-    def return_rows(base, planes, now):
-        back_rows.append(send(base, FO.at[pl.ds(1, 7), planes], RX.at[0, :, planes], below, -1, now))
-        back_rows.append(send(base + 1, FO.at[pl.ds(24, 7), planes], RX.at[1, :, planes], above, 1, now))
+    def return_rows(base, ref, at, planes, now):
+        back_rows.append(send(base, ref.at[pl.ds(1, 7), at], RX.at[0, :, planes], below, -1, now))
+        back_rows.append(send(base + 1, ref.at[pl.ds(24, 7), at], RX.at[1, :, planes], above, 1, now))
 
     def to_depth(number, rows):
         return send(number, F.at[rows, pl.ds(beyond, 8)], RZ.at[rows], (1 - gz, gx, gy))
 
     for start in (1, 24):
         run(start, 1, 7, total)
+    return_rows(18, F, pl.ds(pl.multiple_of(16 * gz, 8), Z - 8), quiet, True)
     margin = [to_depth(16, pl.ds(1, 7)), to_depth(17, pl.ds(24, 7))]
-    for start in (1, 24):
-        run(start, 1, 7, own_planes)
-    return_rows(18, quiet, True)
-    return_rows(20, edge, False)
+    return_rows(20, FO, edge, edge, False)
 
     def inside(step, _):
         k = LEVELS - 1 - step

time: 57.2 us -> 57.2 us (level)
  no operation moved by 1% of the time
where the time goes in v7:
time: 57.2 us; the launch traced here: 57 us
  Pallas kernels  52.8 us (92%)
  between operations  2.4 us (4%)
  local copies, waits for them, and re-layouts  1.81 us (3%)
    pallas_call x1, Pallas kernels, local(): pl.pallas_call(functools.partial(kernel, nx), out_shape=(jax.ShapeDtypeSt...  52.8 us
    unnamed x1, local copies, waits for them, and re-layouts  1.81 us

profile of v7, /device:TPU:32, one launch (start us, length us, event | category | flops | bytes accessed | tf_op | source)
XLA Modules:
  0.0 57.0 jit_solution(1288623800589780934)
XLA Ops:
  0.6 52.8 %shard_map.41 = (f32[16,32,128]{2,1,0:T(8,128)}, f32[1,1]{1,0:T(1,128)}) custom-call(f32[512,128]{1,0:T(8,128)} %bitcast.4, f32[512,128]{1,0:T(8,128)} %bitcast.5), custom_call_target="tpu_custom_call" | custom-call | tf_op jit(solution)/shard_map/pallas_call | solution.py:648
  53.5 1.8 %copy.4 = f32[32,16,128]{2,1,0:T(8,128)} copy(f32[32,16,128]{2,0,1:T(8,128)} %bitcast.6) | data formatting | bytes 524288
